TPU v7x, 1024 devices: a whole 4x4x32 slice. The times are simulated.
1024 devices in a mesh: gx: 32 (over z_hi, y, core), gy: 32 (over z_lo, x).
Axes of the slice: x: 4, y: 4, z: 32 (z_hi: 4, z_lo: 8; z = z_hi * 8 + z_lo), core: 2. Of those that a mesh axis runs over, the one named last changes fastest.
Arguments:
- position: float32 [32, 32, 3, 4096], P('gx', 'gy'), may hold values from 0 to 32, as said below
- velocity: float32 [32, 32, 3, 4096], P('gx', 'gy'), may hold values from -6 to 6
- mass: float32 [32, 32, 1, 4096], P('gx', 'gy'), may hold values from 0.3 to 3
- pair_list: int32 [32, 32, 32, 27], P('gx', 'gy'), may hold values from 0 to 287, as said below
- hot_leaf: int32 [32, 32, 8], P('gx', 'gy'), may hold values from 0 to 32, as said below
Outputs:
- displacement: float32 [32, 32, 3, 4096], P('gx', 'gy')
- new_velocity: float32 [32, 32, 3, 4096], P('gx', 'gy')
Inputs may be any that keep to these rules, and one draw needn't show every extreme that they name: `pair_list`: entry k of every list names a leaf of neighbourhood block k mod 9. `position`: component 0 of a particle of cell (i, j) lies in [i, i + 1), component 1 in [j, j + 1), component 2 in [0, 1). `hot_leaf`: the slots of a cell hold distinct leaf numbers first and the empty mark 32 after them; cell (i, j) and cell (i, (j + 16) mod 32) hold exactly 8 hot leaves together.
All inputs are finite; a program needn't handle non-finite values.
Results may differ from a plain program's by a relative error of at most 0.00023.
Values sent between devices are 32-bit elements; how exact they have to be, the bound alone decides.
No kernel may reach another device: no remote copies, remote signals or barrier semaphores. Data moves between devices by JAX's collectives and lax.ppermute only.
A program may use at most 32 MiB of HBM per device.

v0:
```python
import jax
import jax.numpy as jnp
from jax import lax
from jax.sharding import PartitionSpec as P

LEAF = 128


kernel_scale = 1.0
viscosity = 0.5
time_step = 0.5
base_entries = 9


def with_halo(cells, sides, width):
    for axis, dim in sides:
        count = lax.axis_size(axis)
        ends = count - 1
        head = lax.slice_in_dim(cells, 0, width, axis=dim)
        tail = lax.slice_in_dim(cells, cells.shape[dim] - width, cells.shape[dim], axis=dim)
        cells = jnp.concatenate(
            [
                lax.ppermute(tail, axis, [(i, (i + 1) % count) for i in range(ends)]),
                cells,
                lax.ppermute(head, axis, [((i + 1) % count, i) for i in range(ends)]),
            ],
            axis=dim,
        )
    return cells


def source_leaves(extended):
    channels = extended.shape[2]
    count = extended.shape[3] // LEAF
    return jnp.transpose(extended, (2, 0, 1, 3)).reshape(channels, 9 * count, LEAF)


def own_leaves(own):
    channels = own.shape[0]
    count = own.shape[1] // LEAF
    return jnp.transpose(own.reshape(channels, count, LEAF), (1, 0, 2))


def density_part(target, near):
    diff = target[0:3, :, None] - near[0:3, None, :]
    weight = jnp.exp(-jnp.sum(diff * diff, axis=0) / kernel_scale)
    return jnp.sum(near[6][None, :] * weight, axis=1)


def accel_part(target, target_q, near, near_q):
    diff = target[0:3, :, None] - near[0:3, None, :]
    weight = jnp.exp(-jnp.sum(diff * diff, axis=0) / kernel_scale)
    massed = near[6][None, :] * weight
    press = massed * (2.0 / kernel_scale) * (target_q[:, None] + near_q[None, :])
    pushed = jnp.sum(press[None] * diff, axis=2)
    damped = jnp.sum(
        (massed * near_q[None, :])[None] * (near[3:6, None, :] - target[3:6, :, None]), axis=2
    )
    return pushed + viscosity * damped


def surround_state(state):
    return with_halo(state, (("gx", 0), ("gy", 1)), 1)


def surround_density(inverse):
    return with_halo(inverse, (("gx", 0), ("gy", 1)), 1)


def section(position, velocity, mass, pairs, hot):
    leaf_count = pairs.shape[0]
    slots_all = hot.shape[0]
    own = jnp.concatenate([position, velocity, mass], axis=2)
    extended = surround_state(own)
    sources = source_leaves(extended)
    targets = own_leaves(own[0, 0])
    alive = hot < leaf_count
    alive_float = jnp.where(alive, 1.0, 0.0).astype(jnp.float32)
    slot_leaf = jnp.minimum(hot, leaf_count - 1)
    onehot = jnp.where(
        (slot_leaf[:, None] == jnp.arange(leaf_count, dtype=jnp.int32)[None, :]) & alive[:, None],
        1.0,
        0.0,
    ).astype(jnp.float32)

    def base_density(inputs):
        target, chosen = inputs
        near = jnp.take(sources, chosen, axis=1).reshape(sources.shape[0], -1)
        return density_part(target, near)

    base_rho = lax.map(base_density, (targets, pairs[:, :base_entries]))
    extra_chosen = jnp.take(pairs, slot_leaf, axis=0)[:, base_entries:]
    hot_targets = jnp.take(targets, slot_leaf, axis=0)
    hot_near = jnp.transpose(jnp.take(sources, extra_chosen, axis=1), (1, 0, 2, 3)).reshape(
        slots_all, sources.shape[0], -1
    )
    package = jnp.concatenate([hot_targets, hot_near], axis=2) * alive_float[:, None, None]

    def package_density(pack):
        return density_part(pack[:, :LEAF], pack[:, LEAF:])

    def package_accel(inputs):
        pack, qpack = inputs
        return accel_part(pack[:, :LEAF], qpack[:LEAF], pack[:, LEAF:], qpack[LEAF:])

    extra_rho = lax.map(package_density, package)
    extra_rho = extra_rho * alive_float[:, None]
    added_rho = jnp.dot(onehot.T, extra_rho, precision=lax.Precision.HIGHEST)
    inverse_leaves = 1.0 / (targets[:, 6, :] + base_rho + added_rho)
    inverse = inverse_leaves.reshape(1, -1)
    extended_inverse = surround_density(inverse[None, None])
    source_inverse = source_leaves(extended_inverse)[0]

    def base_accel(inputs):
        target, target_q, chosen = inputs
        near = jnp.take(sources, chosen, axis=1).reshape(sources.shape[0], -1)
        near_q = jnp.take(source_inverse, chosen, axis=0).reshape(-1)
        return accel_part(target, target_q, near, near_q)

    base_acc = lax.map(base_accel, (targets, inverse_leaves, pairs[:, :base_entries]))
    hot_q = jnp.take(inverse_leaves, slot_leaf, axis=0)
    near_q = jnp.take(source_inverse, extra_chosen, axis=0).reshape(slots_all, -1)
    qpackage = jnp.concatenate([hot_q, near_q], axis=1) * alive_float[:, None]
    extra_acc = lax.map(package_accel, (package, qpackage))
    extra_acc = extra_acc * alive_float[:, None, None]
    added_acc = jnp.einsum("hl,hcp->lcp", onehot, extra_acc, precision=lax.Precision.HIGHEST)
    total = base_acc + added_acc
    return jnp.transpose(total, (1, 0, 2)).reshape(3, -1)[None, None]


def local(position, velocity, mass, pair_list, hot_leaf):
    pairs = pair_list[0, 0]
    hot = hot_leaf[0, 0]
    first = section(position, velocity, mass, pairs, hot)
    mid_position = position + 0.5 * time_step * velocity
    mid_velocity = velocity + 0.5 * time_step * first
    second = section(mid_position, mid_velocity, mass, pairs, hot)
    return (time_step * mid_velocity, velocity + time_step * second)


def solution(mesh):
    return jax.shard_map(
        local,
        mesh=mesh,
        in_specs=(
            P("gx", "gy", None, None),
            P("gx", "gy", None, None),
            P("gx", "gy", None, None),
            P("gx", "gy", None, None),
            P("gx", "gy", None),
        ),
        out_specs=(P("gx", "gy", None, None), P("gx", "gy", None, None)),
        check_vma=False,
    )
```

profile of v0, /device:TPU:896, one launch (start us, length us, event | category | flops | bytes accessed | tf_op | source)
XLA Modules:
  0.0 442.8 jit_solution(10430459357298252409)
XLA Ops:
  1.7 10.3 %collective-permute-start.1 = (f32[1,1,7,4096]{3,1,2,0:T(1,128)S(1)}, f32[1,1,7,4096]{3,1,2,0:T(1,128)S(1)}, u32[]{:S(2)}, u32[]{:S(2)}) collective-permute-start(f32[1,1,7,4096]{3,1,2,0:T(1,128)S(1)} %pad_maximum_fusion.6), channel_id=1, source_target_pairs={{32,0},{64,32},{96,64},{128,96},{160,128},{192,160},{224,192},{256... | collective-permute-start | bytes 344072 | tf_op jit(solution)/shard_map/ppermute | solution.py:25
  18.2 11.0 %collective-permute-done = f32[1,1,7,4096]{3,1,2,0:T(1,128)S(1)} collective-permute-done((f32[1,1,7,4096]{3,1,2,0:T(1,128)S(1)}, f32[1,1,7,4096]{3,1,2,0:T(1,128)S(1)}, u32[]{:S(2)}, u32[]{:S(2)}) %collective-permute-start) | collective-permute-done | bytes 114720 | tf_op jit(solution)/shard_map/ppermute | solution.py:23
  30.4 13.3 %collective-permute-start.3 = (f32[3,1,7,4096]{3,1,2,0:T(1,128)S(1)}, f32[3,1,7,4096]{3,1,2,0:T(1,128)S(1)}, u32[]{:S(2)}, u32[]{:S(2)}) collective-permute-start(f32[3,1,7,4096]{3,1,2,0:T(1,128)S(1)} %pad_maximum_fusion.2), channel_id=1, source_target_pairs={{1,0},{2,1},{3,2},{4,3},{5,4},{6,5},{7,6},{8,7},{9,8},{10,9},{11,1... | collective-permute-start | bytes 1032200 | tf_op jit(solution)/shard_map/ppermute | solution.py:25
  45.9 2.6 collective-permute-done.3
  48.5 7.7 %collective-permute-done.2 = f32[3,1,7,4096]{3,1,2,0:T(1,128)S(1)} collective-permute-done((f32[3,1,7,4096]{3,1,2,0:T(1,128)S(1)}, f32[3,1,7,4096]{3,1,2,0:T(1,128)S(1)}, u32[]{:S(2)}, u32[]{:S(2)}) %collective-permute-start.2) | collective-permute-done | bytes 344096 | tf_op jit(solution)/shard_map/ppermute | solution.py:23
  58.9 38.7 %while.80 = (s32[]{:T(128)}, f32[32,128]{1,0:T(8,128)S(1)}, s32[32,9]{1,0:T(8,128)S(1)}, f32[7,288,128]{2,0,1:T(8,128)S(1)}, f32[32,7,128]{2,1,0:T(8,128)S(1)}, /*index=5*/s32[]{:T(128)}, s32[]{:T(128)}) while((s32[]{:T(128)}, f32[32,128]{1,0:T(8,128)S(1)}, s32[32,9]{1,0:T(8,128)S(1)}, f32[7,288,128]{2,0,1:T(8,128)S(1)}, ...), condition=%wide.region_3.5_spmd, body=%wide.region_0.4_spmd.sunk | while | flops 1631032 | bytes 1381635 | solution.py:91
  99.0 6.5 %while.81 = (s32[]{:T(128)}, f32[8,128]{1,0:T(8,128)S(1)}, f32[8,7,2432]{2,1,0:T(8,128)S(1)}, s32[]{:T(128)}, s32[]{:T(128)}) while((s32[]{:T(128)}, f32[8,128]{1,0:T(8,128)S(1)}, f32[8,7,2432]{2,1,0:T(8,128)S(1)}, s32[]{:T(128)}, s32[]{:T(128)}) %tuple.217), condition=%wide.region_7.12_spmd, body=%wide.region_4.11_spmd.sunk | while | flops 3243906 | bytes 2612301 | solution.py:106
  110.8 12.9 %collective-permute-done.4 = f32[1,1,1,4096]{3,2,1,0:T(1,128)S(1)} collective-permute-done((f32[1,1,1,4096]{3,2,1,0:T(1,128)S(1)}, f32[1,1,1,4096]{3,2,1,0:T(1,128)S(1)}, u32[]{:S(2)}, u32[]{:S(2)}) %collective-permute-start.4) | collective-permute-done | bytes 16416 | tf_op jit(solution)/shard_map/ppermute | solution.py:23
  125.7 3.9 collective-permute-start.6
  129.8 5.2 %collective-permute-done.6 = f32[3,1,1,4096]{3,2,1,0:T(1,128)S(1)} collective-permute-done((f32[3,1,1,4096]{3,2,1,0:T(1,128)S(1)}, f32[3,1,1,4096]{3,2,1,0:T(1,128)S(1)}, u32[]{:S(2)}, u32[]{:S(2)}) %collective-permute-start.6) | collective-permute-done | bytes 49184 | tf_op jit(solution)/shard_map/ppermute | solution.py:23
  135.8 77.3 %while.82 = (s32[]{:T(128)}, f32[32,3,128]{2,0,1:T(8,128)S(1)}, s32[32,9]{1,0:T(8,128)S(1)}, f32[7,288,128]{2,0,1:T(8,128)S(1)}, f32[32,7,128]{2,1,0:T(8,128)S(1...) while((s32[]{:T(128)}, f32[32,3,128]{2,0,1:T(8,128)S(1)}, ...), condition=%wide.region_12.18_spmd, body=%wide.region_8.17_spmd.sunk | while | flops 4728888 | bytes 3839300 | solution.py:120
  213.4 15.2 %while.83 = (s32[]{:T(128)}, f32[8,3,128]{2,1,0:T(4,128)S(1)}, f32[8,7,2432]{2,1,0:T(8,128)S(1)}, f32[8,2432]{1,0:T(8,128)S(1)}, s32[]{:T(128)}, /*index=5*/s32[]{:T(128)}, s32[]{}) while((s32[]{:T(128)}, f32[8,3,128]{2,1,0:T(4,128)S(1)}, f32[8,7,2432]{2,1,0:T(8,128)S(1)}, f32[8,2432]{1,0:T(8,128)S(1)}, s32[]{:T(128)}, ...), condition=%wide.region_17.25_spmd, body=%wide.region_13.24_spmd.sunk | while | flops 9437187 | bytes 7484533 | solution.py:124
  231.1 2.4 collective-permute-start.8
  233.6 17.2 %collective-permute-done.8 = f32[1,1,7,4096]{3,2,1,0:T(8,128)S(1)} collective-permute-done((f32[1,1,7,4096]{3,2,1,0:T(8,128)S(1)}, f32[1,1,7,4096]{3,2,1,0:T(8,128)S(1)}, u32[]{:S(2)}, u32[]{:S(2)}) %collective-permute-start.8) | collective-permute-done | bytes 114720 | tf_op jit(solution)/shard_map/ppermute | solution.py:23
  250.8 8.0 %collective-permute-start.11 = (f32[3,1,7,4096]{3,2,1,0:T(8,128)S(1)}, f32[3,1,7,4096]{3,2,1,0:T(8,128)S(1)}, u32[]{:S(2)}, u32[]{:S(2)}) collective-permute-start(f32[3,1,7,4096]{3,2,1,0:T(8,128)S(1)} %pad_maximum_fusion.1), channel_id=1, source_target_pairs={{1,0},{2,1},{3,2},{4,3},{5,4},{6,5},{7,6},{8,7},{9,8},{10,9},{11,1... | collective-permute-start | bytes 1032200 | tf_op jit(solution)/shard_map/ppermute | solution.py:25
  264.1 7.7 %collective-permute-done.10 = f32[3,1,7,4096]{3,2,1,0:T(8,128)S(1)} collective-permute-done((f32[3,1,7,4096]{3,2,1,0:T(8,128)S(1)}, f32[3,1,7,4096]{3,2,1,0:T(8,128)S(1)}, u32[]{:S(2)}, u32[]{:S(2)}) %collective-permute-start.10) | collective-permute-done | bytes 344096 | tf_op jit(solution)/shard_map/ppermute | solution.py:23
  272.8 38.7 %while.84 = (s32[]{:T(128)}, f32[32,128]{1,0:T(8,128)S(1)}, s32[32,9]{1,0:T(8,128)S(1)}, f32[7,288,128]{2,0,1:T(8,128)S(1)}, f32[32,7,128]{2,1,0:T(8,128)S(1)}, /*index=5*/s32[]{:T(128)}, s32[]{:T(128)}) while((s32[]{:T(128)}, f32[32,128]{1,0:T(8,128)S(1)}, s32[32,9]{1,0:T(8,128)S(1)}, f32[7,288,128]{2,0,1:T(8,128)S(1)}, ...), condition=%wide.region_21.29_spmd, body=%wide.region_18.28_spmd.sunk | while | flops 1631032 | bytes 1381635 | solution.py:91
  312.1 6.5 %while.85 = (s32[]{:T(128)}, f32[8,128]{1,0:T(8,128)S(1)}, f32[8,7,2432]{2,1,0:T(8,128)S(1)}, s32[]{:T(128)}, s32[]{:T(128)}) while((s32[]{:T(128)}, f32[8,128]{1,0:T(8,128)S(1)}, f32[8,7,2432]{2,1,0:T(8,128)S(1)}, s32[]{:T(128)}, s32[]{:T(128)}) %tuple.229), condition=%wide.region_25.33_spmd, body=%wide.region_22.32_spmd.sunk | while | flops 3243906 | bytes 2612301 | solution.py:106
  320.9 2.4 collective-permute-start.12
  324.6 12.2 %collective-permute-done.12 = f32[1,1,1,4096]{3,2,1,0:T(1,128)S(1)} collective-permute-done((f32[1,1,1,4096]{3,2,1,0:T(1,128)S(1)}, f32[1,1,1,4096]{3,2,1,0:T(1,128)S(1)}, u32[]{:S(2)}, u32[]{:S(2)}) %collective-permute-start.12) | collective-permute-done | bytes 16416 | tf_op jit(solution)/shard_map/ppermute | solution.py:23
  338.8 3.9 collective-permute-start.14
  342.8 5.2 %collective-permute-done.14 = f32[3,1,1,4096]{3,2,1,0:T(1,128)S(1)} collective-permute-done((f32[3,1,1,4096]{3,2,1,0:T(1,128)S(1)}, f32[3,1,1,4096]{3,2,1,0:T(1,128)S(1)}, u32[]{:S(2)}, u32[]{:S(2)}) %collective-permute-start.14) | collective-permute-done | bytes 49184 | tf_op jit(solution)/shard_map/ppermute | solution.py:23
  348.9 77.3 %while.86 = (s32[]{:T(128)}, f32[32,3,128]{2,0,1:T(8,128)S(1)}, s32[32,9]{1,0:T(8,128)S(1)}, f32[7,288,128]{2,0,1:T(8,128)S(1)}, f32[32,7,128]{2,1,0:T(8,128)S(1...) while((s32[]{:T(128)}, f32[32,3,128]{2,0,1:T(8,128)S(1)}, ...), condition=%wide.region_30.38_spmd, body=%wide.region_26.37_spmd.sunk | while | flops 4728888 | bytes 3839300 | solution.py:120
  426.5 15.2 %while.87 = (s32[]{:T(128)}, f32[8,3,128]{2,1,0:T(4,128)S(1)}, f32[8,7,2432]{2,1,0:T(8,128)S(1)}, f32[8,2432]{1,0:T(8,128)S(1)}, s32[]{:T(128)}, /*index=5*/s32[]{:T(128)}, s32[]{}) while((s32[]{:T(128)}, f32[8,3,128]{2,1,0:T(4,128)S(1)}, f32[8,7,2432]{2,1,0:T(8,128)S(1)}, f32[8,2432]{1,0:T(8,128)S(1)}, s32[]{:T(128)}, ...), condition=%wide.region_35.43_spmd, body=%wide.region_31.42_spmd.sunk | while | flops 9437187 | bytes 7484533 | solution.py:124
  (2167 shorter events, 300.9 us)
Async XLA Ops:
  0.6 55.6 %copy-start.2 = (f32[1,1,1,4096]{3,2,1,0:T(1,128)S(1)}, f32[1,1,1,4096]{3,2,1,0:T(1,128)}, u32[]{:S(2)}) copy-start(f32[1,1,1,4096]{3,2,1,0:T(1,128)} %param.37) | copy-start | bytes 49156
  0.6 55.6 %copy-start = (f32[1,1,3,4096]{3,1,2,0:T(1,128)S(1)}, f32[1,1,3,4096]{3,1,2,0:T(1,128)}, u32[]{:S(2)}) copy-start(f32[1,1,3,4096]{3,1,2,0:T(1,128)} %param.36) | copy-start | bytes 147460
  0.7 55.6 %copy-start.1 = (f32[1,1,3,4096]{3,1,2,0:T(1,128)S(1)}, f32[1,1,3,4096]{3,1,2,0:T(1,128)}, u32[]{:S(2)}) copy-start(f32[1,1,3,4096]{3,1,2,0:T(1,128)} %param.35) | copy-start | bytes 147460
  0.7 45.0 %copy-start.3 = (s32[1,1,8]{2,1,0:T(1,128)S(1)}, s32[1,1,8]{2,1,0:T(1,128)}, u32[]{:S(2)}) copy-start(s32[1,1,8]{2,1,0:T(1,128)} %param.39) | copy-start | bytes 100
  1.7 16.5 %collective-permute-start.1 = (f32[1,1,7,4096]{3,1,2,0:T(1,128)S(1)}, f32[1,1,7,4096]{3,1,2,0:T(1,128)S(1)}, u32[]{:S(2)}, u32[]{:S(2)}) collective-permute-start(f32[1,1,7,4096]{3,1,2,0:T(1,128)S(1)} %pad_maximum_fusion.6), channel_id=1, source_target_pairs={{32,0},{64,32},{96,64},{128,96},{160,128},{192,160},{224,192},{256... | collective-permute-start | bytes 344072 | tf_op jit(solution)/shard_map/ppermute | solution.py:25
  12.0 17.2 %collective-permute-start = (f32[1,1,7,4096]{3,1,2,0:T(1,128)S(1)}, f32[1,1,7,4096]{3,1,2,0:T(1,128)S(1)}, u32[]{:S(2)}, u32[]{:S(2)}) collective-permute-start(f32[1,1,7,4096]{3,1,2,0:T(1,128)S(1)} %pad_maximum_fusion.6), channel_id=1, source_target_pairs={{0,32},{32,64},{64,96},{96,128},{128,160},{160,192},{192,224},{224... | collective-permute-start | bytes 344072 | tf_op jit(solution)/shard_map/ppermute | solution.py:23
  30.4 18.1 %collective-permute-start.3 = (f32[3,1,7,4096]{3,1,2,0:T(1,128)S(1)}, f32[3,1,7,4096]{3,1,2,0:T(1,128)S(1)}, u32[]{:S(2)}, u32[]{:S(2)}) collective-permute-start(f32[3,1,7,4096]{3,1,2,0:T(1,128)S(1)} %pad_maximum_fusion.2), channel_id=1, source_target_pairs={{1,0},{2,1},{3,2},{4,3},{5,4},{6,5},{7,6},{8,7},{9,8},{10,9},{11,1... | collective-permute-start | bytes 1032200 | tf_op jit(solution)/shard_map/ppermute | solution.py:25
  43.7 12.5 %collective-permute-start.2 = (f32[3,1,7,4096]{3,1,2,0:T(1,128)S(1)}, f32[3,1,7,4096]{3,1,2,0:T(1,128)S(1)}, u32[]{:S(2)}, u32[]{:S(2)}) collective-permute-start(f32[3,1,7,4096]{3,1,2,0:T(1,128)S(1)} %pad_maximum_fusion.2), channel_id=1, source_target_pairs={{0,1},{1,2},{2,3},{3,4},{4,5},{5,6},{6,7},{7,8},{8,9},{9,10},{10,1... | collective-permute-start | bytes 1032200 | tf_op jit(solution)/shard_map/ppermute | solution.py:23
  105.9 4.9 %collective-permute-start.5 = (f32[1,1,1,4096]{3,2,1,0:T(1,128)S(1)}, f32[1,1,1,4096]{3,2,1,0:T(1,128)S(1)}, u32[]{:S(2)}, u32[]{:S(2)}) collective-permute-start(f32[1,1,1,4096]{3,2,1,0:T(1,128)S(1)} %bitcast.260), channel_id=1, source_target_pairs={{32,0},{64,32},{96,64},{128,96},{160,128},{192,160},{224,192},{256... | collective-permute-start | bytes 49160 | tf_op jit(solution)/shard_map/ppermute | solution.py:25
  107.8 15.9 %collective-permute-start.4 = (f32[1,1,1,4096]{3,2,1,0:T(1,128)S(1)}, f32[1,1,1,4096]{3,2,1,0:T(1,128)S(1)}, u32[]{:S(2)}, u32[]{:S(2)}) collective-permute-start(f32[1,1,1,4096]{3,2,1,0:T(1,128)S(1)} %bitcast.261), channel_id=1, source_target_pairs={{0,32},{32,64},{64,96},{96,128},{128,160},{160,192},{192,224},{224... | collective-permute-start | bytes 49160 | tf_op jit(solution)/shard_map/ppermute | solution.py:23
  123.8 6.0 %collective-permute-start.7 = (f32[3,1,1,4096]{3,2,1,0:T(1,128)S(1)}, f32[3,1,1,4096]{3,2,1,0:T(1,128)S(1)}, u32[]{:S(2)}, u32[]{:S(2)}) collective-permute-start(f32[3,1,1,4096]{3,2,1,0:T(1,128)S(1)} %pad_maximum_fusion.7), channel_id=1, source_target_pairs={{1,0},{2,1},{3,2},{4,3},{5,4},{6,5},{7,6},{8,7},{9,8},{10,9},{11,1... | collective-permute-start | bytes 147464 | tf_op jit(solution)/shard_map/ppermute | solution.py:25
  125.7 9.3 %collective-permute-start.6 = (f32[3,1,1,4096]{3,2,1,0:T(1,128)S(1)}, f32[3,1,1,4096]{3,2,1,0:T(1,128)S(1)}, u32[]{:S(2)}, u32[]{:S(2)}) collective-permute-start(f32[3,1,1,4096]{3,2,1,0:T(1,128)S(1)} %pad_maximum_fusion.7), channel_id=1, source_target_pairs={{0,1},{1,2},{2,3},{3,4},{4,5},{5,6},{6,7},{7,8},{8,9},{9,10},{10,1... | collective-permute-start | bytes 147464 | tf_op jit(solution)/shard_map/ppermute | solution.py:23
  229.1 4.4 collective-permute-start.9
  231.1 19.7 %collective-permute-start.8 = (f32[1,1,7,4096]{3,2,1,0:T(8,128)S(1)}, f32[1,1,7,4096]{3,2,1,0:T(8,128)S(1)}, u32[]{:S(2)}, u32[]{:S(2)}) collective-permute-start(f32[1,1,7,4096]{3,2,1,0:T(8,128)S(1)} %pad_maximum_fusion.5), channel_id=1, source_target_pairs={{0,32},{32,64},{64,96},{96,128},{128,160},{160,192},{192,224},{224... | collective-permute-start | bytes 344072 | tf_op jit(solution)/shard_map/ppermute | solution.py:23
  250.8 13.3 %collective-permute-start.11 = (f32[3,1,7,4096]{3,2,1,0:T(8,128)S(1)}, f32[3,1,7,4096]{3,2,1,0:T(8,128)S(1)}, u32[]{:S(2)}, u32[]{:S(2)}) collective-permute-start(f32[3,1,7,4096]{3,2,1,0:T(8,128)S(1)} %pad_maximum_fusion.1), channel_id=1, source_target_pairs={{1,0},{2,1},{3,2},{4,3},{5,4},{6,5},{7,6},{8,7},{9,8},{10,9},{11,1... | collective-permute-start | bytes 1032200 | tf_op jit(solution)/shard_map/ppermute | solution.py:25
  258.8 13.0 %collective-permute-start.10 = (f32[3,1,7,4096]{3,2,1,0:T(8,128)S(1)}, f32[3,1,7,4096]{3,2,1,0:T(8,128)S(1)}, u32[]{:S(2)}, u32[]{:S(2)}) collective-permute-start(f32[3,1,7,4096]{3,2,1,0:T(8,128)S(1)} %pad_maximum_fusion.1), channel_id=1, source_target_pairs={{0,1},{1,2},{2,3},{3,4},{4,5},{5,6},{6,7},{7,8},{8,9},{9,10},{10,1... | collective-permute-start | bytes 1032200 | tf_op jit(solution)/shard_map/ppermute | solution.py:23
  319.0 5.6 %collective-permute-start.13 = (f32[1,1,1,4096]{3,2,1,0:T(1,128)S(1)}, f32[1,1,1,4096]{3,2,1,0:T(1,128)S(1)}, u32[]{:S(2)}, u32[]{:S(2)}) collective-permute-start(f32[1,1,1,4096]{3,2,1,0:T(1,128)S(1)} %bitcast.256), channel_id=1, source_target_pairs={{32,0},{64,32},{96,64},{128,96},{160,128},{192,160},{224,192},{256... | collective-permute-start | bytes 49160 | tf_op jit(solution)/shard_map/ppermute | solution.py:25
  320.9 15.9 %collective-permute-start.12 = (f32[1,1,1,4096]{3,2,1,0:T(1,128)S(1)}, f32[1,1,1,4096]{3,2,1,0:T(1,128)S(1)}, u32[]{:S(2)}, u32[]{:S(2)}) collective-permute-start(f32[1,1,1,4096]{3,2,1,0:T(1,128)S(1)} %bitcast.257), channel_id=1, source_target_pairs={{0,32},{32,64},{64,96},{96,128},{128,160},{160,192},{192,224},{224... | collective-permute-start | bytes 49160 | tf_op jit(solution)/shard_map/ppermute | solution.py:23
  336.8 6.0 %collective-permute-start.15 = (f32[3,1,1,4096]{3,2,1,0:T(1,128)S(1)}, f32[3,1,1,4096]{3,2,1,0:T(1,128)S(1)}, u32[]{:S(2)}, u32[]{:S(2)}) collective-permute-start(f32[3,1,1,4096]{3,2,1,0:T(1,128)S(1)} %pad_maximum_fusion.8), channel_id=1, source_target_pairs={{1,0},{2,1},{3,2},{4,3},{5,4},{6,5},{7,6},{8,7},{9,8},{10,9},{11,1... | collective-permute-start | bytes 147464 | tf_op jit(solution)/shard_map/ppermute | solution.py:25
  338.8 9.3 %collective-permute-start.14 = (f32[3,1,1,4096]{3,2,1,0:T(1,128)S(1)}, f32[3,1,1,4096]{3,2,1,0:T(1,128)S(1)}, u32[]{:S(2)}, u32[]{:S(2)}) collective-permute-start(f32[3,1,1,4096]{3,2,1,0:T(1,128)S(1)} %pad_maximum_fusion.8), channel_id=1, source_target_pairs={{0,1},{1,2},{2,3},{3,4},{4,5},{5,6},{6,7},{7,8},{8,9},{9,10},{10,1... | collective-permute-start | bytes 147464 | tf_op jit(solution)/shard_map/ppermute | solution.py:23
where the time goes:
time: 444 us; the launch traced here: 443 us
  other arithmetic  146 us (33%)
  local copies, waits for them, and re-layouts  133 us (30%)
  waiting for transfers between devices  84.6 us (19%)
  starting transfers between devices  62.3 us (14%)
  loops' own time  14.4 us (3%)
    ppermute x8, waiting for transfers between devices, with_halo(): lax.ppermute(tail, axis, [(i, (i + 1) % count) for i in range(ends)])  79.3 us
    reduce_sum x80, other arithmetic, accel_part(): pushed = jnp.sum(press[None] * diff, axis=2)  47.5 us
    ppermute x8, starting transfers between devices, with_halo(): lax.ppermute(head, axis, [((i + 1) % count, i) for i in range(ends)])  41.3 us
    gather x64, local copies, waits for them, and re-layouts, base_accel(): near_q = jnp.take(source_inverse, chosen, axis=0).reshape(-1)  35.6 us
    gather x64, local copies, waits for them, and re-layouts, base_accel(): near = jnp.take(sources, chosen, axis=1).reshape(sources.shape[0], -1)  35.6 us
    gather x64, local copies, waits for them, and re-layouts, base_density(): near = jnp.take(sources, chosen, axis=1).reshape(sources.shape[0], -1)  35.6 us
    reduce_sum x80, other arithmetic, density_part(): weight = jnp.exp(-jnp.sum(diff * diff, axis=0) / kernel_scale)  21.7 us
    reduce_sum x80, other arithmetic, accel_part(): weight = jnp.exp(-jnp.sum(diff * diff, axis=0) / kernel_scale)  21.7 us
  transfers between devices with their start and end apart: 16, of which 13 were waited for; matrix products, arithmetic and copies ran while one was open for 2% of the time, Pallas kernels for 0%

commit v1 on v0

v1 whole, which is shorter than its diff:
```python
import functools
import math
import jax
import jax.numpy as jnp
from jax import lax
from jax.experimental import pallas as pl
from jax.experimental.pallas import tpu as pltpu
from jax.sharding import PartitionSpec as P

LEAF = 128
CELLS = 9
BASE = 9
time_step = 0.5
F32 = jnp.float32
BF16 = jnp.bfloat16
ROOT = math.sqrt(math.log2(math.e))
VM = 56 * 2**20


def halves(a):
    hi = a.astype(BF16)
    return hi, (a - hi.astype(F32)).astype(BF16)


def thirds(a):
    hi = a.astype(BF16).astype(F32)
    rest = a - hi
    mid = rest.astype(BF16).astype(F32)
    return hi, mid, rest - mid


def columns_of(e_ref, origin_ref, cell, start, width, drift):
    r = e_ref[cell, :, pl.ds(start, width)]
    x = r[0:3] - origin_ref[0:3, 0:1]
    v = r[3:6]
    if drift:
        x = x + drift * v
    return x, v, r[6:7]


def prepare_sources(e_ref, origin_ref, s_ref, drift, slot, width=1024):
    leaves = e_ref.shape[2] // LEAF
    per = width // LEAF

    def step(i, _):
        cell = i // (leaves // per)
        part = i % (leaves // per)
        x, _, m = columns_of(e_ref, origin_ref, cell, pl.multiple_of(part * width, width), width, drift)
        y = x * ROOT
        c = jnp.where(m > 0, jnp.log2(m), -1000.0) - jnp.sum(y * y, axis=0, keepdims=True)
        h, d, l = thirds(jnp.concatenate([2.0 * y, c, jnp.ones_like(c), jnp.zeros_like(y)], axis=0))
        g = jnp.concatenate([h, d, h, l], axis=0).astype(BF16)
        for k in range(per):
            s_ref[(slot + cell) * leaves + part * per + k] = g[:, k * LEAF:(k + 1) * LEAF]
        return 0

    lax.fori_loop(0, e_ref.shape[0] * leaves // per, step, 0)


def target_rows(e_ref, origin_ref, drift):
    width = e_ref.shape[2]
    x, _, _ = columns_of(e_ref, origin_ref, 0, 0, width, drift)
    y = x * ROOT
    n = -jnp.sum(y * y, axis=0, keepdims=True)
    h, d, l = thirds(jnp.concatenate([y, jnp.ones_like(n), n, jnp.zeros_like(y)], axis=0))
    z = jnp.zeros_like(h)
    return jnp.concatenate([h, h, d, d, l, h, z, z], axis=0).astype(BF16)


def source_rows(s_ref, leaf):
    s = s_ref[leaf]
    return jnp.concatenate([s[0:16], s[0:16], s[16:32], s[16:32]], axis=0)


def weights(s_ref, t, chosen):
    s = jnp.concatenate([source_rows(s_ref, leaf)[0:48] for leaf in chosen], axis=1)
    return jnp.exp2(jnp.dot(t, s, preferred_element_type=F32))


def against(a, b):
    return lax.dot_general(a, b, (((1,), (1,)), ((), ())), preferred_element_type=F32)


def groups(begin, end, size=2):
    return [range(k, min(k + size, end)) for k in range(begin, end, size)]


def every_leaf(hot_ref, leaves, entries, group, together, part, store, add):
    def base(i, _):
        for g in range(group):
            store(i * group + g, part(i * group + g, 0, BASE))
        return 0

    lax.fori_loop(0, leaves // group, base, 0)
    for begin in range(0, hot_ref.shape[0], together):
        @pl.when(hot_ref[begin] < leaves)
        def _():
            for slot in range(begin, begin + together):
                leaf = jnp.minimum(hot_ref[slot], leaves - 1)
                alive = jnp.where(hot_ref[slot] < leaves, 1.0, 0.0)
                add(leaf, alive * part(leaf, BASE, entries))


def density_kernel(drift, group, together, pair_ref, hot_ref, e_ref, e1_ref, e2_ref, origin_ref, q_ref, s_ref, t_ref, sum_ref):
    leaves = e_ref.shape[2] // LEAF
    for i, ref in enumerate((e_ref, e1_ref, e2_ref)):
        prepare_sources(ref, origin_ref, s_ref, drift, 3 * i)
    rows = target_rows(e_ref, origin_ref, drift)
    for leaf in range(leaves):
        t = rows[:, leaf * LEAF:(leaf + 1) * LEAF]
        t_ref[leaf] = jnp.concatenate([t, t], axis=0).T

    def part(leaf, begin, end):
        t = t_ref[leaf][:, 0:48]
        total = jnp.zeros((LEAF, LEAF), F32)
        for ks in groups(begin, end):
            w = weights(s_ref, t, [pair_ref[leaf, k] for k in ks])
            for i in range(len(ks)):
                total = total + w[:, i * LEAF:(i + 1) * LEAF]
        return total

    def store(leaf, value):
        sum_ref[leaf] = value

    def add(leaf, value):
        sum_ref[leaf] = sum_ref[leaf] + value

    every_leaf(hot_ref, leaves, pair_ref.shape[1], group, together, part, store, add)
    ones = jnp.ones((8, 3 * LEAF), BF16)
    for leaf in range(leaves):
        at = slice(leaf * LEAF, (leaf + 1) * LEAF)
        total = jnp.concatenate([a.astype(BF16) for a in thirds(sum_ref[leaf])], axis=1)
        q_ref[0:1, at] = 1.0 / (e_ref[0, 6:7, at] + against(ones, total)[0:1])


def density(drift, pairs, hot, extended, origin, group=16, together=4):
    part = extended[0].shape[2]
    leaves = part // LEAF
    return pl.pallas_call(
        functools.partial(density_kernel, drift, group, together),
        out_shape=(
            jax.ShapeDtypeStruct((1, part), F32),
            jax.ShapeDtypeStruct((CELLS * leaves, 32, LEAF), BF16),
        ),
        in_specs=[pl.BlockSpec(memory_space=pltpu.SMEM)] * 2 + [pl.BlockSpec(memory_space=pltpu.VMEM)] * 4,
        out_specs=[pl.BlockSpec(memory_space=pltpu.VMEM)] * 2,
        scratch_shapes=[pltpu.VMEM((leaves, LEAF, LEAF), BF16), pltpu.VMEM((leaves, LEAF, LEAF), F32)],
        compiler_params=pltpu.CompilerParams(vmem_limit_bytes=VM),
        name="density",
    )(pairs, hot, *extended, origin)


def prepare_moments(e_ref, v_ref, origin_ref, g_ref, drift, slot, width=1024):
    leaves = e_ref.shape[2] // LEAF
    per = width // LEAF

    def step(i, _):
        cell = i // (leaves // per)
        part = i % (leaves // per)
        start = pl.multiple_of(part * width, width)
        x, v, _ = columns_of(e_ref, origin_ref, cell, start, width, drift)
        if drift:
            v = v_ref[cell, 0:3, pl.ds(start, width)]
            q = v_ref[cell, 3:4, pl.ds(start, width)]
        else:
            q = v_ref[cell, :, pl.ds(start, width)]
        z = jnp.zeros_like(q)
        g = jnp.concatenate([q * x, q, z, x, q * v, z, z, z, z, z], axis=0)
        both = jnp.concatenate(halves(g), axis=0)
        for k in range(per):
            g_ref[(slot + cell) * leaves + part * per + k] = both[:, k * LEAF:(k + 1) * LEAF]
        return 0

    lax.fori_loop(0, e_ref.shape[0] * leaves // per, step, 0)


def accel_kernel(drift, group, together, pair_ref, hot_ref, e_ref, e1_ref, e2_ref, v_ref, v1_ref, v2_ref, s_ref, origin_ref, acc_ref, t_ref, g_ref, sum_ref):
    leaves = e_ref.shape[2] // LEAF
    for i, refs in enumerate(((e_ref, v_ref), (e1_ref, v1_ref), (e2_ref, v2_ref))):
        prepare_moments(*refs, origin_ref, g_ref, drift, 3 * i)

    t_ref[...] = target_rows(e_ref, origin_ref, drift)

    def part(leaf, begin, end):
        t = t_ref[:, pl.ds(pl.multiple_of(leaf * LEAF, LEAF), LEAF)]
        z = jnp.zeros_like(t)
        two = jnp.concatenate([jnp.concatenate([t, z], axis=1), jnp.concatenate([z, t], axis=1)], axis=0)
        total = jnp.zeros((32, 2 * LEAF), F32)
        for ks in groups(begin, end):
            n = len(ks)
            chosen = [pair_ref[leaf, k] for k in ks]
            s = jnp.concatenate([source_rows(s_ref, c) for c in (chosen + chosen)[0:2]], axis=0).T
            hi, lo = halves(jnp.exp2(jnp.dot(s, two if n == 2 else two[:, :LEAF], preferred_element_type=F32)))
            at = [slice(i * LEAF, (i + 1) * LEAF) for i in range(n)]
            r = jnp.concatenate([jnp.concatenate([hi[:, a], lo[:, a]], axis=1) for a in at], axis=0)
            g = jnp.concatenate([g_ref[c] for c in chosen], axis=1)
            total = total + jnp.dot(g, r, preferred_element_type=F32)
        return total[0:16, :LEAF] + (total[0:16, LEAF:] + (total[16:32, :LEAF] + total[16:32, LEAF:]))

    def store(leaf, value):
        sum_ref[leaf] = value

    def add(leaf, value):
        sum_ref[leaf] = sum_ref[leaf] + value

    every_leaf(hot_ref, leaves, pair_ref.shape[1], group, together, part, store, add)
    for leaf in range(leaves):
        at = slice(leaf * LEAF, (leaf + 1) * LEAF)
        x, v, m = columns_of(e_ref, origin_ref, 0, leaf * LEAF, LEAF, drift)
        if drift:
            v, q = v_ref[0, 0:3, at], v_ref[0, 3:4, at]
        else:
            q = v_ref[0, :, at]
        s0 = 1.0 / q - m
        o = sum_ref[leaf]
        s3, s2, s1, s4 = o[0:3], o[3:4], o[5:8], o[8:11]
        acc_ref[:, at] = 2.0 * (q * (x * s0 - s1) + (x * s2 - s3)) + 0.5 * (s4 - v * s2)


def accel(drift, pairs, hot, extended, fresh, kept, origin, group=16, together=4):
    part = extended[0].shape[2]
    leaves = part // LEAF
    return pl.pallas_call(
        functools.partial(accel_kernel, drift, group, together),
        out_shape=jax.ShapeDtypeStruct((3, part), F32),
        in_specs=[pl.BlockSpec(memory_space=pltpu.SMEM)] * 2 + [pl.BlockSpec(memory_space=pltpu.VMEM)] * 8,
        out_specs=pl.BlockSpec(memory_space=pltpu.VMEM),
        scratch_shapes=[
            pltpu.VMEM((64, part), BF16),
            pltpu.VMEM((CELLS * leaves, 32, LEAF), BF16),
            pltpu.VMEM((leaves, 16, LEAF), F32),
        ],
        compiler_params=pltpu.CompilerParams(vmem_limit_bytes=VM),
        name="accel",
    )(pairs, hot, *extended, *fresh, *kept, origin)


def swaps(cells, axis):
    count = lax.axis_size(axis)
    got = []
    for first in (0, 1):
        pairs = [(i, i + 1) for i in range(first, count - 1, 2)]
        got.append(lax.ppermute(cells, axis, pairs + [(b, a) for a, b in pairs]))
    return got


def surround(own):
    here = jnp.stack([own] + swaps(own, "gx"))
    return [here] + swaps(here, "gy")


def slot_of(block_step, axis):
    even = lax.axis_index(axis) % 2 == 0
    return jnp.where(block_step == 1, 0, jnp.where((block_step == 2) == even, 1, 2))


def to_slots(pairs, leaves):
    block = pairs // leaves
    return (3 * slot_of(block % 3, "gy") + slot_of(block // 3, "gx")) * leaves + pairs % leaves


def cell_origin():
    row = lax.axis_index("gx").astype(F32) + 0.5
    column = lax.axis_index("gy").astype(F32) + 0.5
    middle = jnp.stack([row, column, jnp.full_like(row, 0.5)] + [jnp.zeros_like(row)] * 5)
    return jnp.broadcast_to(middle[:, None], (8, LEAF))


def local(position, velocity, mass, pair_list, hot_leaf):
    pairs = to_slots(pair_list[0, 0], pair_list.shape[2])
    hot = hot_leaf[0, 0]
    half = 0.5 * time_step
    origin = cell_origin()
    speed = velocity[0, 0]
    extended = surround(jnp.concatenate([position[0, 0], speed, mass[0, 0]], axis=0))
    first_inverse, *first_kept = density(0.0, pairs, hot, extended, origin)
    second_inverse, *second_kept = density(half, pairs, hot, extended, origin)
    first = accel(0.0, pairs, hot, extended, surround(first_inverse), first_kept, origin)
    mid_speed = speed + half * first
    later = surround(jnp.concatenate([mid_speed, second_inverse], axis=0))
    second = accel(half, pairs, hot, extended, later, second_kept, origin)
    return ((time_step * mid_speed)[None, None], (speed + time_step * second)[None, None])


def solution(mesh):
    return jax.shard_map(
        local,
        mesh=mesh,
        in_specs=(
            P("gx", "gy", None, None),
            P("gx", "gy", None, None),
            P("gx", "gy", None, None),
            P("gx", "gy", None, None),
            P("gx", "gy", None),
        ),
        out_specs=(P("gx", "gy", None, None), P("gx", "gy", None, None)),
        check_vma=False,
    )
```

time: 444 us -> 156 us (0.35)
  the two profiles are of different devices: /device:TPU:896 before, /device:TPU:870 now
where the time goes in v1:
time: 156 us; the launch traced here: 155 us
  Pallas kernels  53.2 us (34%)
  waiting for transfers between devices  49.7 us (32%)
  starting transfers between devices  42 us (27%)
  local copies, waits for them, and re-layouts  5.2 us (3%)
  other arithmetic  4.11 us (3%)
    ppermute x12, waiting for transfers between devices, swaps(): got.append(lax.ppermute(cells, axis, pairs + [(b, a) for a, b in pairs]))  49.7 us
    ppermute x12, starting transfers between devices, swaps(): got.append(lax.ppermute(cells, axis, pairs + [(b, a) for a, b in pairs]))  42 us
    pallas_call x2, Pallas kernels, accel(): pl.pallas_call(functools.partial(accel_kernel, drift, group, together), o...  30.4 us
    pallas_call x2, Pallas kernels, density(): pl.pallas_call(functools.partial(density_kernel, drift, group, together),...  22.8 us
    unnamed x26, local copies, waits for them, and re-layouts  4.34 us
  transfers between devices with their start and end apart: 12, of which 7 were waited for; matrix products, arithmetic and copies ran while one was open for 1% of the time, Pallas kernels for 7%

profile of v1, /device:TPU:870, one launch (start us, length us, event | category | flops | bytes accessed | tf_op | source)
XLA Modules:
  0.0 155.0 jit_solution(11014367594943097441)
XLA Ops:
  0.6 0.9 copy_bitcast_fusion
  2.3 10.3 %collective-permute-start.1 = (f32[7,4096]{1,0:T(8,128)S(1)}, f32[7,4096]{1,0:T(8,128)S(1)}, u32[]{:S(2)}, u32[]{:S(2)}) collective-permute-start(f32[7,4096]{1,0:T(8,128)S(1)} %pad_maximum_fusion.2), channel_id=1, source_target_pairs={{32,64},{96,128},{160,192},{224,256},{288,320},{352,384},{416,448}... | collective-permute-start | bytes 344072 | tf_op jit(solution)/shard_map/ppermute | solution.py:243
  12.6 1.9 %collective-permute-start = (f32[7,4096]{1,0:T(8,128)S(1)}, f32[7,4096]{1,0:T(8,128)S(1)}, u32[]{:S(2)}, u32[]{:S(2)}) collective-permute-start(f32[7,4096]{1,0:T(8,128)S(1)} %pad_maximum_fusion.2), channel_id=1, source_target_pairs={{0,32},{64,96},{128,160},{192,224},{256,288},{320,352},{384,416},{... | collective-permute-start | bytes 344072 | tf_op jit(solution)/shard_map/ppermute | solution.py:243
  14.6 11.9 %collective-permute-done.1 = f32[7,4096]{1,0:T(8,128)S(1)} collective-permute-done((f32[7,4096]{1,0:T(8,128)S(1)}, f32[7,4096]{1,0:T(8,128)S(1)}, u32[]{:S(2)}, u32[]{:S(2)}) %collective-permute-start.1) | collective-permute-done | bytes 114720 | tf_op jit(solution)/shard_map/ppermute | solution.py:243
  26.5 2.7 %collective-permute-start.2 = (f32[3,7,4096]{2,1,0:T(8,128)S(1)}, f32[3,7,4096]{2,1,0:T(8,128)S(1)}, u32[]{:S(2)}, u32[]{:S(2)}) collective-permute-start(f32[3,7,4096]{2,1,0:T(8,128)S(1)} %pad_maximum_fusion.e_ref), channel_id=1, source_target_pairs={{0,1},{2,3},{4,5},{6,7},{8,9},{10,11},{12,13},{14,15},{16,17},{18,... | collective-permute-start | bytes 1032200 | tf_op jit(solution)/shard_map/ppermute | solution.py:243
  29.2 1.9 %collective-permute-start.3 = (f32[3,7,4096]{2,1,0:T(8,128)S(1)}, f32[3,7,4096]{2,1,0:T(8,128)S(1)}, u32[]{:S(2)}, u32[]{:S(2)}) collective-permute-start(f32[3,7,4096]{2,1,0:T(8,128)S(1)} %pad_maximum_fusion.e_ref), channel_id=1, source_target_pairs={{1,2},{3,4},{5,6},{7,8},{9,10},{11,12},{13,14},{15,16},{17,18},{19... | collective-permute-start | bytes 1032200 | tf_op jit(solution)/shard_map/ppermute | solution.py:243
  32.7 3.5 %collective-permute-done.2.e1_ref = f32[3,7,4096]{2,1,0:T(8,128)S(1)} collective-permute-done((f32[3,7,4096]{2,1,0:T(8,128)S(1)}, f32[3,7,4096]{2,1,0:T(8,128)S(1)}, u32[]{:S(2)}, u32[]{:S(2)}) %collective-permute-start.2) | collective-permute-done | bytes 344096 | tf_op jit(solution)/shard_map/ppermute | solution.py:243
  36.2 6.0 %collective-permute-done.3.e2_ref = f32[3,7,4096]{2,1,0:T(8,128)S(1)} collective-permute-done((f32[3,7,4096]{2,1,0:T(8,128)S(1)}, f32[3,7,4096]{2,1,0:T(8,128)S(1)}, u32[]{:S(2)}, u32[]{:S(2)}) %collective-permute-start.3) | collective-permute-done | bytes 344096 | tf_op jit(solution)/shard_map/ppermute | solution.py:243
  43.0 11.3 %density.2 = (f32[1,4096]{1,0:T(1,128)}, bf16[288,32,128]{2,1,0:T(8,128)(2,1)}) custom-call(s32[32,27]{1,0:T(8,128)} %fusion.pair_ref, s32[8]{0:T(128)} %bitcast.54, f32[3,7,4096]{2,1,0:T(8,128)} %copy-done, f32[3,7,4096]{2,1,0:T(8,128)} %copy-done.1, f32[3,7,4096]{2,1,0:T(8,128)} %copy-done.2, f32[8,128]{1,0:T(8,128)} %broadcast_in_dim.21.origin_ref), custom_call_target="tpu_custom_call" | custom-call | tf_op jit(solution)/shard_map/density/pallas_call | solution.py:139
  54.2 7.0 %collective-permute-start.5 = (f32[1,4096]{1,0:T(1,128)}, f32[1,4096]{1,0:T(1,128)S(1)}, u32[]{:S(2)}, u32[]{:S(2)}) collective-permute-start(f32[1,4096]{1,0:T(1,128)} %get-tuple-element.6), channel_id=1, source_target_pairs={{32,64},{96,128},{160,192},{224,256},{288,320},{352,384},{416,448}... | collective-permute-start | bytes 49160 | tf_op jit(solution)/shard_map/ppermute | solution.py:243
  61.3 1.9 %collective-permute-start.4 = (f32[1,4096]{1,0:T(1,128)}, f32[1,4096]{1,0:T(1,128)S(1)}, u32[]{:S(2)}, u32[]{:S(2)}) collective-permute-start(f32[1,4096]{1,0:T(1,128)} %get-tuple-element.6), channel_id=1, source_target_pairs={{0,32},{64,96},{128,160},{192,224},{256,288},{320,352},{384,416},{... | collective-permute-start | bytes 49160 | tf_op jit(solution)/shard_map/ppermute | solution.py:243
  63.2 7.1 %collective-permute-done.5 = f32[1,4096]{1,0:T(1,128)S(1)} collective-permute-done((f32[1,4096]{1,0:T(1,128)}, f32[1,4096]{1,0:T(1,128)S(1)}, u32[]{:S(2)}, u32[]{:S(2)}) %collective-permute-start.5) | collective-permute-done | bytes 16416 | tf_op jit(solution)/shard_map/ppermute | solution.py:243
  71.1 2.1 %collective-permute-start.6 = (f32[3,1,4096]{2,1,0:T(1,128)S(1)}, f32[3,1,4096]{2,1,0:T(1,128)S(1)}, u32[]{:S(2)}, u32[]{:S(2)}) collective-permute-start(f32[3,1,4096]{2,1,0:T(1,128)S(1)} %pad_maximum_fusion.4.v_ref), channel_id=1, source_target_pairs={{0,1},{2,3},{4,5},{6,7},{8,9},{10,11},{12,13},{14,15},{16,17},{18,... | collective-permute-start | bytes 147464 | tf_op jit(solution)/shard_map/ppermute | solution.py:243
  73.2 1.9 %collective-permute-start.7 = (f32[3,1,4096]{2,1,0:T(1,128)S(1)}, f32[3,1,4096]{2,1,0:T(1,128)S(1)}, u32[]{:S(2)}, u32[]{:S(2)}) collective-permute-start(f32[3,1,4096]{2,1,0:T(1,128)S(1)} %pad_maximum_fusion.4.v_ref), channel_id=1, source_target_pairs={{1,2},{3,4},{5,6},{7,8},{9,10},{11,12},{13,14},{15,16},{17,18},{19... | collective-permute-start | bytes 147464 | tf_op jit(solution)/shard_map/ppermute | solution.py:243
  75.1 11.5 %density.3 = (f32[1,4096]{1,0:T(1,128)}, bf16[288,32,128]{2,1,0:T(8,128)(2,1)}) custom-call(s32[32,27]{1,0:T(8,128)} %fusion.pair_ref, s32[8]{0:T(128)} %bitcast.55, f32[3,7,4096]{2,1,0:T(8,128)} %copy-done, f32[3,7,4096]{2,1,0:T(8,128)} %copy-done.1, f32[3,7,4096]{2,1,0:T(8,128)} %copy-done.2, f32[8,128]{1,0:T(8,128)} %broadcast_in_dim.21.origin_ref), custom_call_target="tpu_custom_call" | custom-call | tf_op jit(solution)/shard_map/density/pallas_call | solution.py:139
  87.3 15.0 %accel.2 = f32[3,4096]{1,0:T(4,128)} custom-call(s32[32,27]{1,0:T(8,128)} %fusion.pair_ref, s32[8]{0:T(128)} %bitcast.56, f32[3,7,4096]{2,1,0:T(8,128)} %copy-done, f32[3,7,4096]{2,1,0:T(8,128)} %copy-done.1, f32[3,7,4096]{2,1,0:T(8,128)} %copy-done.2, f32[3,1,4096]{2,1,0:T(1,128)} %copy-done.5, f32[3,1,4096]{2,1,0:T(1,128)} %copy-done.9, ...), custom_call_target="tpu_custom_call" | custom-call | tf_op jit(solution)/shard_map/accel/pallas_call | solution.py:223
  103.3 5.5 %collective-permute-start.9 = (f32[4,4096]{1,0:T(4,128)S(1)}, f32[4,4096]{1,0:T(4,128)S(1)}, u32[]{:S(2)}, u32[]{:S(2)}) collective-permute-start(f32[4,4096]{1,0:T(4,128)S(1)} %pad_maximum_fusion.3), channel_id=1, source_target_pairs={{32,64},{96,128},{160,192},{224,256},{288,320},{352,384},{416,448}... | collective-permute-start | bytes 196616 | tf_op jit(solution)/shard_map/ppermute | solution.py:243
  108.8 1.9 %collective-permute-start.8 = (f32[4,4096]{1,0:T(4,128)S(1)}, f32[4,4096]{1,0:T(4,128)S(1)}, u32[]{:S(2)}, u32[]{:S(2)}) collective-permute-start(f32[4,4096]{1,0:T(4,128)S(1)} %pad_maximum_fusion.3), channel_id=1, source_target_pairs={{0,32},{64,96},{128,160},{192,224},{256,288},{320,352},{384,416},{... | collective-permute-start | bytes 196616 | tf_op jit(solution)/shard_map/ppermute | solution.py:243
  110.8 13.3 %collective-permute-done.9 = f32[4,4096]{1,0:T(4,128)S(1)} collective-permute-done((f32[4,4096]{1,0:T(4,128)S(1)}, f32[4,4096]{1,0:T(4,128)S(1)}, u32[]{:S(2)}, u32[]{:S(2)}) %collective-permute-start.9) | collective-permute-done | bytes 65568 | tf_op jit(solution)/shard_map/ppermute | solution.py:243
  124.1 2.4 %collective-permute-start.10 = (f32[3,4,4096]{2,1,0:T(4,128)S(1)}, f32[3,4,4096]{2,1,0:T(4,128)S(1)}, u32[]{:S(2)}, u32[]{:S(2)}) collective-permute-start(f32[3,4,4096]{2,1,0:T(4,128)S(1)} %pad_maximum_fusion.1.v_ref), channel_id=1, source_target_pairs={{0,1},{2,3},{4,5},{6,7},{8,9},{10,11},{12,13},{14,15},{16,17},{18,... | collective-permute-start | bytes 589832 | tf_op jit(solution)/shard_map/ppermute | solution.py:243
  126.6 2.3 %collective-permute-start.11 = (f32[3,4,4096]{2,1,0:T(4,128)S(1)}, f32[3,4,4096]{2,1,0:T(4,128)S(1)}, u32[]{:S(2)}, u32[]{:S(2)}) collective-permute-start(f32[3,4,4096]{2,1,0:T(4,128)S(1)} %pad_maximum_fusion.1.v_ref), channel_id=1, source_target_pairs={{1,2},{3,4},{5,6},{7,8},{9,10},{11,12},{13,14},{15,16},{17,18},{19... | collective-permute-start | bytes 589832 | tf_op jit(solution)/shard_map/ppermute | solution.py:243
  129.6 2.1 %collective-permute-done.10.v1_ref = f32[3,4,4096]{2,1,0:T(4,128)S(1)} collective-permute-done((f32[3,4,4096]{2,1,0:T(4,128)S(1)}, f32[3,4,4096]{2,1,0:T(4,128)S(1)}, u32[]{:S(2)}, u32[]{:S(2)}) %collective-permute-start.10) | collective-permute-done | bytes 196640 | tf_op jit(solution)/shard_map/ppermute | solution.py:243
  131.7 5.8 %collective-permute-done.11.v2_ref = f32[3,4,4096]{2,1,0:T(4,128)S(1)} collective-permute-done((f32[3,4,4096]{2,1,0:T(4,128)S(1)}, f32[3,4,4096]{2,1,0:T(4,128)S(1)}, u32[]{:S(2)}, u32[]{:S(2)}) %collective-permute-start.11) | collective-permute-done | bytes 196640 | tf_op jit(solution)/shard_map/ppermute | solution.py:243
  138.1 15.3 %accel.3 = f32[3,4096]{1,0:T(4,128)} custom-call(s32[32,27]{1,0:T(8,128)} %fusion.pair_ref, s32[8]{0:T(128)} %bitcast.57, f32[3,7,4096]{2,1,0:T(8,128)} %copy-done, f32[3,7,4096]{2,1,0:T(8,128)} %copy-done.1, f32[3,7,4096]{2,1,0:T(8,128)} %copy-done.2, f32[3,4,4096]{2,1,0:T(4,128)} %copy-done.3, f32[3,4,4096]{2,1,0:T(4,128)} %copy-done.6, ...), custom_call_target="tpu_custom_call" | custom-call | tf_op jit(solution)/shard_map/accel/pallas_call | solution.py:223
  (42 shorter events, 8.4 us)
Async XLA Ops:
  2.3 24.2 %collective-permute-start.1 = (f32[7,4096]{1,0:T(8,128)S(1)}, f32[7,4096]{1,0:T(8,128)S(1)}, u32[]{:S(2)}, u32[]{:S(2)}) collective-permute-start(f32[7,4096]{1,0:T(8,128)S(1)} %pad_maximum_fusion.2), channel_id=1, source_target_pairs={{32,64},{96,128},{160,192},{224,256},{288,320},{352,384},{416,448}... | collective-permute-start | bytes 344072 | tf_op jit(solution)/shard_map/ppermute | solution.py:243
  12.6 13.8 %collective-permute-start = (f32[7,4096]{1,0:T(8,128)S(1)}, f32[7,4096]{1,0:T(8,128)S(1)}, u32[]{:S(2)}, u32[]{:S(2)}) collective-permute-start(f32[7,4096]{1,0:T(8,128)S(1)} %pad_maximum_fusion.2), channel_id=1, source_target_pairs={{0,32},{64,96},{128,160},{192,224},{256,288},{320,352},{384,416},{... | collective-permute-start | bytes 344072 | tf_op jit(solution)/shard_map/ppermute | solution.py:243
  26.5 16.4 %copy-start = (f32[3,7,4096]{2,1,0:T(8,128)}, f32[3,7,4096]{2,1,0:T(8,128)S(1)}, u32[]{:S(2)}) copy-start(f32[3,7,4096]{2,1,0:T(8,128)S(1)} %pad_maximum_fusion.e_ref) | copy-start | bytes 1032196
  26.5 9.7 %collective-permute-start.2 = (f32[3,7,4096]{2,1,0:T(8,128)S(1)}, f32[3,7,4096]{2,1,0:T(8,128)S(1)}, u32[]{:S(2)}, u32[]{:S(2)}) collective-permute-start(f32[3,7,4096]{2,1,0:T(8,128)S(1)} %pad_maximum_fusion.e_ref), channel_id=1, source_target_pairs={{0,1},{2,3},{4,5},{6,7},{8,9},{10,11},{12,13},{14,15},{16,17},{18,... | collective-permute-start | bytes 1032200 | tf_op jit(solution)/shard_map/ppermute | solution.py:243
  29.2 13.0 %collective-permute-start.3 = (f32[3,7,4096]{2,1,0:T(8,128)S(1)}, f32[3,7,4096]{2,1,0:T(8,128)S(1)}, u32[]{:S(2)}, u32[]{:S(2)}) collective-permute-start(f32[3,7,4096]{2,1,0:T(8,128)S(1)} %pad_maximum_fusion.e_ref), channel_id=1, source_target_pairs={{1,2},{3,4},{5,6},{7,8},{9,10},{11,12},{13,14},{15,16},{17,18},{19... | collective-permute-start | bytes 1032200 | tf_op jit(solution)/shard_map/ppermute | solution.py:243
  36.2 6.8 %copy-start.1 = (f32[3,7,4096]{2,1,0:T(8,128)}, f32[3,7,4096]{2,1,0:T(8,128)S(1)}, u32[]{:S(2)}) copy-start(f32[3,7,4096]{2,1,0:T(8,128)S(1)} %collective-permute-done.2.e1_ref) | copy-start | bytes 1032196
  42.2 0.8 copy-start.2
  54.2 16.1 %collective-permute-start.5 = (f32[1,4096]{1,0:T(1,128)}, f32[1,4096]{1,0:T(1,128)S(1)}, u32[]{:S(2)}, u32[]{:S(2)}) collective-permute-start(f32[1,4096]{1,0:T(1,128)} %get-tuple-element.6), channel_id=1, source_target_pairs={{32,64},{96,128},{160,192},{224,256},{288,320},{352,384},{416,448}... | collective-permute-start | bytes 49160 | tf_op jit(solution)/shard_map/ppermute | solution.py:243
  61.3 9.0 %collective-permute-start.4 = (f32[1,4096]{1,0:T(1,128)}, f32[1,4096]{1,0:T(1,128)S(1)}, u32[]{:S(2)}, u32[]{:S(2)}) collective-permute-start(f32[1,4096]{1,0:T(1,128)} %get-tuple-element.6), channel_id=1, source_target_pairs={{0,32},{64,96},{128,160},{192,224},{256,288},{320,352},{384,416},{... | collective-permute-start | bytes 49160 | tf_op jit(solution)/shard_map/ppermute | solution.py:243
  71.1 15.6 %copy-start.5 = (f32[3,1,4096]{2,1,0:T(1,128)}, f32[3,1,4096]{2,1,0:T(1,128)S(1)}, u32[]{:S(2)}) copy-start(f32[3,1,4096]{2,1,0:T(1,128)S(1)} %pad_maximum_fusion.4.v_ref) | copy-start | bytes 147460
  71.1 31.2 %copy-start.4 = (f32[1,1,3,4096]{3,1,2,0:T(1,128)S(1)}, f32[1,1,3,4096]{3,1,2,0:T(1,128)}, u32[]{:S(2)}) copy-start(f32[1,1,3,4096]{3,1,2,0:T(1,128)} %param.6) | copy-start | bytes 147460
  71.1 15.5 %collective-permute-start.6 = (f32[3,1,4096]{2,1,0:T(1,128)S(1)}, f32[3,1,4096]{2,1,0:T(1,128)S(1)}, u32[]{:S(2)}, u32[]{:S(2)}) collective-permute-start(f32[3,1,4096]{2,1,0:T(1,128)S(1)} %pad_maximum_fusion.4.v_ref), channel_id=1, source_target_pairs={{0,1},{2,3},{4,5},{6,7},{8,9},{10,11},{12,13},{14,15},{16,17},{18,... | collective-permute-start | bytes 147464 | tf_op jit(solution)/shard_map/ppermute | solution.py:243
  73.2 13.5 %collective-permute-start.7 = (f32[3,1,4096]{2,1,0:T(1,128)S(1)}, f32[3,1,4096]{2,1,0:T(1,128)S(1)}, u32[]{:S(2)}, u32[]{:S(2)}) collective-permute-start(f32[3,1,4096]{2,1,0:T(1,128)S(1)} %pad_maximum_fusion.4.v_ref), channel_id=1, source_target_pairs={{1,2},{3,4},{5,6},{7,8},{9,10},{11,12},{13,14},{15,16},{17,18},{19... | collective-permute-start | bytes 147464 | tf_op jit(solution)/shard_map/ppermute | solution.py:243
  86.6 16.6 %copy-start.8 = (f32[1,4096]{1,0:T(1,128)S(1)}, f32[1,4096]{1,0:T(1,128)}, u32[]{:S(2)}) copy-start(f32[1,4096]{1,0:T(1,128)} %get-tuple-element.8) | copy-start | bytes 49156
  86.6 0.6 copy-start.9
  86.6 0.6 copy-start.10
  103.3 20.8 %collective-permute-start.9 = (f32[4,4096]{1,0:T(4,128)S(1)}, f32[4,4096]{1,0:T(4,128)S(1)}, u32[]{:S(2)}, u32[]{:S(2)}) collective-permute-start(f32[4,4096]{1,0:T(4,128)S(1)} %pad_maximum_fusion.3), channel_id=1, source_target_pairs={{32,64},{96,128},{160,192},{224,256},{288,320},{352,384},{416,448}... | collective-permute-start | bytes 196616 | tf_op jit(solution)/shard_map/ppermute | solution.py:243
  108.8 15.3 %collective-permute-start.8 = (f32[4,4096]{1,0:T(4,128)S(1)}, f32[4,4096]{1,0:T(4,128)S(1)}, u32[]{:S(2)}, u32[]{:S(2)}) collective-permute-start(f32[4,4096]{1,0:T(4,128)S(1)} %pad_maximum_fusion.3), channel_id=1, source_target_pairs={{0,32},{64,96},{128,160},{192,224},{256,288},{320,352},{384,416},{... | collective-permute-start | bytes 196616 | tf_op jit(solution)/shard_map/ppermute | solution.py:243
  124.1 13.3 %copy-start.3 = (f32[3,4,4096]{2,1,0:T(4,128)}, f32[3,4,4096]{2,1,0:T(4,128)S(1)}, u32[]{:S(2)}) copy-start(f32[3,4,4096]{2,1,0:T(4,128)S(1)} %pad_maximum_fusion.1.v_ref) | copy-start | bytes 589828
  124.1 7.6 %collective-permute-start.10 = (f32[3,4,4096]{2,1,0:T(4,128)S(1)}, f32[3,4,4096]{2,1,0:T(4,128)S(1)}, u32[]{:S(2)}, u32[]{:S(2)}) collective-permute-start(f32[3,4,4096]{2,1,0:T(4,128)S(1)} %pad_maximum_fusion.1.v_ref), channel_id=1, source_target_pairs={{0,1},{2,3},{4,5},{6,7},{8,9},{10,11},{12,13},{14,15},{16,17},{18,... | collective-permute-start | bytes 589832 | tf_op jit(solution)/shard_map/ppermute | solution.py:243
  126.6 10.9 %collective-permute-start.11 = (f32[3,4,4096]{2,1,0:T(4,128)S(1)}, f32[3,4,4096]{2,1,0:T(4,128)S(1)}, u32[]{:S(2)}, u32[]{:S(2)}) collective-permute-start(f32[3,4,4096]{2,1,0:T(4,128)S(1)} %pad_maximum_fusion.1.v_ref), channel_id=1, source_target_pairs={{1,2},{3,4},{5,6},{7,8},{9,10},{11,12},{13,14},{15,16},{17,18},{19... | collective-permute-start | bytes 589832 | tf_op jit(solution)/shard_map/ppermute | solution.py:243
  131.7 5.8 %copy-start.6 = (f32[3,4,4096]{2,1,0:T(4,128)}, f32[3,4,4096]{2,1,0:T(4,128)S(1)}, u32[]{:S(2)}) copy-start(f32[3,4,4096]{2,1,0:T(4,128)S(1)} %collective-permute-done.10.v1_ref) | copy-start | bytes 589828
  137.4 0.7 copy-start.7

commit v2 on v1

--- a/solution.py
+++ b/solution.py
@@ -11,10 +11,11 @@
 CELLS = 9
 BASE = 9
 time_step = 0.5
+viscosity = 0.5
 F32 = jnp.float32
 BF16 = jnp.bfloat16
 ROOT = math.sqrt(math.log2(math.e))
-VM = 56 * 2**20
+VM = 24 * 2**20
 
 
 def halves(a):
@@ -29,26 +30,40 @@
     return hi, mid, rest - mid
 
 
-def columns_of(e_ref, origin_ref, cell, start, width, drift):
-    r = e_ref[cell, :, pl.ds(start, width)]
-    x = r[0:3] - origin_ref[0:3, 0:1]
-    v = r[3:6]
+def row_index(width):
+    return lax.broadcasted_iota(jnp.int32, (8, width), 0)
+
+
+def eight(a):
+    return jnp.concatenate([a, jnp.zeros((8 - a.shape[0], a.shape[1]), a.dtype)], axis=0)
+
+
+def centred(state, origin_ref, drift):
+    r = eight(state)
+    row = row_index(r.shape[1])
+    x = r - jnp.where(row == 0, origin_ref[0], jnp.where(row == 1, origin_ref[1], 0.5))
     if drift:
-        x = x + drift * v
-    return x, v, r[6:7]
+        x = x + drift * pltpu.roll(r, 5, 0)
+    return jnp.where(row < 3, x, r)
+
+
+def squared(x, row):
+    y = x * ROOT
+    return y, jnp.sum(jnp.where(row < 3, y * y, 0.0), axis=0, keepdims=True)
 
 
 def prepare_sources(e_ref, origin_ref, s_ref, drift, slot, width=1024):
     leaves = e_ref.shape[2] // LEAF
     per = width // LEAF
+    row = row_index(width)
 
     def step(i, _):
         cell = i // (leaves // per)
         part = i % (leaves // per)
-        x, _, m = columns_of(e_ref, origin_ref, cell, pl.multiple_of(part * width, width), width, drift)
-        y = x * ROOT
-        c = jnp.where(m > 0, jnp.log2(m), -1000.0) - jnp.sum(y * y, axis=0, keepdims=True)
-        h, d, l = thirds(jnp.concatenate([2.0 * y, c, jnp.ones_like(c), jnp.zeros_like(y)], axis=0))
+        r = centred(e_ref[cell, :, pl.ds(pl.multiple_of(part * width, width), width)], origin_ref, drift)
+        y, size = squared(r, row)
+        c = jnp.where(r > 0, jnp.log2(r), -1000.0) - size
+        h, d, l = thirds(jnp.where(row < 3, 2.0 * y, jnp.where(row == 3, 1.0, jnp.where(row == 6, c, 0.0))))
         g = jnp.concatenate([h, d, h, l], axis=0).astype(BF16)
         for k in range(per):
             s_ref[(slot + cell) * leaves + part * per + k] = g[:, k * LEAF:(k + 1) * LEAF]
@@ -58,11 +73,10 @@
 
 
 def target_rows(e_ref, origin_ref, drift):
-    width = e_ref.shape[2]
-    x, _, _ = columns_of(e_ref, origin_ref, 0, 0, width, drift)
-    y = x * ROOT
-    n = -jnp.sum(y * y, axis=0, keepdims=True)
-    h, d, l = thirds(jnp.concatenate([y, jnp.ones_like(n), n, jnp.zeros_like(y)], axis=0))
+    r = centred(e_ref[0], origin_ref, drift)
+    row = row_index(r.shape[1])
+    y, size = squared(r, row)
+    h, d, l = thirds(jnp.where(row < 3, y, jnp.where(row == 3, -size, jnp.where(row == 6, 1.0, 0.0))))
     z = jnp.zeros_like(h)
     return jnp.concatenate([h, h, d, d, l, h, z, z], axis=0).astype(BF16)
 
@@ -101,7 +115,7 @@
                 add(leaf, alive * part(leaf, BASE, entries))
 
 
-def density_kernel(drift, group, together, pair_ref, hot_ref, e_ref, e1_ref, e2_ref, origin_ref, q_ref, s_ref, t_ref, sum_ref):
+def density_kernel(drift, group, together, pair_ref, hot_ref, origin_ref, e_ref, e1_ref, e2_ref, q_ref, s_ref, t_ref, sum_ref):
     leaves = e_ref.shape[2] // LEAF
     for i, ref in enumerate((e_ref, e1_ref, e2_ref)):
         prepare_sources(ref, origin_ref, s_ref, drift, 3 * i)
@@ -133,7 +147,7 @@
         q_ref[0:1, at] = 1.0 / (e_ref[0, 6:7, at] + against(ones, total)[0:1])
 
 
-def density(drift, pairs, hot, extended, origin, group=16, together=4):
+def density(drift, pairs, hot, origin, extended, group=32, together=8):
     part = extended[0].shape[2]
     leaves = part // LEAF
     return pl.pallas_call(
@@ -142,31 +156,32 @@
             jax.ShapeDtypeStruct((1, part), F32),
             jax.ShapeDtypeStruct((CELLS * leaves, 32, LEAF), BF16),
         ),
-        in_specs=[pl.BlockSpec(memory_space=pltpu.SMEM)] * 2 + [pl.BlockSpec(memory_space=pltpu.VMEM)] * 4,
+        in_specs=[pl.BlockSpec(memory_space=pltpu.SMEM)] * 3 + [pl.BlockSpec(memory_space=pltpu.VMEM)] * 3,
         out_specs=[pl.BlockSpec(memory_space=pltpu.VMEM)] * 2,
         scratch_shapes=[pltpu.VMEM((leaves, LEAF, LEAF), BF16), pltpu.VMEM((leaves, LEAF, LEAF), F32)],
         compiler_params=pltpu.CompilerParams(vmem_limit_bytes=VM),
         name="density",
-    )(pairs, hot, *extended, origin)
+    )(pairs, hot, origin, *extended)
 
 
 def prepare_moments(e_ref, v_ref, origin_ref, g_ref, drift, slot, width=1024):
     leaves = e_ref.shape[2] // LEAF
     per = width // LEAF
+    row = row_index(width)
 
     def step(i, _):
         cell = i // (leaves // per)
         part = i % (leaves // per)
-        start = pl.multiple_of(part * width, width)
-        x, v, _ = columns_of(e_ref, origin_ref, cell, start, width, drift)
+        at = pl.ds(pl.multiple_of(part * width, width), width)
+        r = centred(e_ref[cell, :, at], origin_ref, drift)
         if drift:
-            v = v_ref[cell, 0:3, pl.ds(start, width)]
-            q = v_ref[cell, 3:4, pl.ds(start, width)]
+            fresh = v_ref[cell, :, at]
+            q = fresh[3:4]
+            r = jnp.where(row < 3, r, pltpu.roll(eight(fresh), 3, 0))
         else:
-            q = v_ref[cell, :, pl.ds(start, width)]
-        z = jnp.zeros_like(q)
-        g = jnp.concatenate([q * x, q, z, x, q * v, z, z, z, z, z], axis=0)
-        both = jnp.concatenate(halves(g), axis=0)
+            q = v_ref[cell, :, at]
+        r = jnp.where(row < 6, r, 1.0)
+        both = jnp.concatenate(halves(jnp.concatenate([q * r, r], axis=0)), axis=0)
         for k in range(per):
             g_ref[(slot + cell) * leaves + part * per + k] = both[:, k * LEAF:(k + 1) * LEAF]
         return 0
@@ -174,11 +189,14 @@
     lax.fori_loop(0, e_ref.shape[0] * leaves // per, step, 0)
 
 
-def accel_kernel(drift, group, together, pair_ref, hot_ref, e_ref, e1_ref, e2_ref, v_ref, v1_ref, v2_ref, s_ref, origin_ref, acc_ref, t_ref, g_ref, sum_ref):
+def accel_kernel(drift, group, together, pair_ref, hot_ref, origin_ref, e_ref, e1_ref, e2_ref, v_ref, v1_ref, v2_ref, s_ref, *rest):
+    if drift:
+        out_ref, t_ref, g_ref, sum_ref = rest
+    else:
+        next_ref, out_ref, mid_ref, t_ref, g_ref, sum_ref = rest
     leaves = e_ref.shape[2] // LEAF
     for i, refs in enumerate(((e_ref, v_ref), (e1_ref, v1_ref), (e2_ref, v2_ref))):
         prepare_moments(*refs, origin_ref, g_ref, drift, 3 * i)
-
     t_ref[...] = target_rows(e_ref, origin_ref, drift)
 
     def part(leaf, begin, end):
@@ -204,27 +222,39 @@
         sum_ref[leaf] = sum_ref[leaf] + value
 
     every_leaf(hot_ref, leaves, pair_ref.shape[1], group, together, part, store, add)
+    half = 0.5 * time_step
     for leaf in range(leaves):
         at = slice(leaf * LEAF, (leaf + 1) * LEAF)
-        x, v, m = columns_of(e_ref, origin_ref, 0, leaf * LEAF, LEAF, drift)
+        r = centred(e_ref[0, :, at], origin_ref, drift)
+        x, m, speed = r[0:3], r[6:7], r[3:6]
         if drift:
             v, q = v_ref[0, 0:3, at], v_ref[0, 3:4, at]
         else:
-            q = v_ref[0, :, at]
-        s0 = 1.0 / q - m
+            v, q = speed, v_ref[0, :, at]
         o = sum_ref[leaf]
-        s3, s2, s1, s4 = o[0:3], o[3:4], o[5:8], o[8:11]
-        acc_ref[:, at] = 2.0 * (q * (x * s0 - s1) + (x * s2 - s3)) + 0.5 * (s4 - v * s2)
-
-
-def accel(drift, pairs, hot, extended, fresh, kept, origin, group=16, together=4):
+        s3, s4, s2, s1 = o[0:3], o[3:6], o[6:7], o[8:11]
+        acc = 2.0 * (q * (x * (1.0 / q - m) - s1) + (x * s2 - s3)) + viscosity * (s4 - v * s2)
+        if drift:
+            out = speed + time_step * acc
+        else:
+            mid = speed + half * acc
+            mid_ref[0:3, at] = mid
+            mid_ref[3:4, at] = next_ref[0:1, at]
+            out = time_step * mid
+        for i in range(3):
+            out_ref[i, 0:1, at] = out[i:i + 1]
+
+
+def accel(drift, pairs, hot, origin, extended, fresh, kept, following=None, group=32, together=8):
     part = extended[0].shape[2]
     leaves = part // LEAF
+    out = jax.ShapeDtypeStruct((3, 1, part), F32)
+    more = [] if drift else [following]
     return pl.pallas_call(
         functools.partial(accel_kernel, drift, group, together),
-        out_shape=jax.ShapeDtypeStruct((3, part), F32),
-        in_specs=[pl.BlockSpec(memory_space=pltpu.SMEM)] * 2 + [pl.BlockSpec(memory_space=pltpu.VMEM)] * 8,
-        out_specs=pl.BlockSpec(memory_space=pltpu.VMEM),
+        out_shape=out if drift else (out, jax.ShapeDtypeStruct((4, part), F32)),
+        in_specs=[pl.BlockSpec(memory_space=pltpu.SMEM)] * 3 + [pl.BlockSpec(memory_space=pltpu.VMEM)] * (7 + len(more)),
+        out_specs=pl.BlockSpec(memory_space=pltpu.VMEM) if drift else [pl.BlockSpec(memory_space=pltpu.VMEM)] * 2,
         scratch_shapes=[
             pltpu.VMEM((64, part), BF16),
             pltpu.VMEM((CELLS * leaves, 32, LEAF), BF16),
@@ -232,7 +262,7 @@
         ],
         compiler_params=pltpu.CompilerParams(vmem_limit_bytes=VM),
         name="accel",
-    )(pairs, hot, *extended, *fresh, *kept, origin)
+    )(pairs, hot, origin, *extended, *fresh, kept, *more)
 
 
 def swaps(cells, axis):
@@ -259,27 +289,21 @@
     return (3 * slot_of(block % 3, "gy") + slot_of(block // 3, "gx")) * leaves + pairs % leaves
 
 
-def cell_origin():
-    row = lax.axis_index("gx").astype(F32) + 0.5
-    column = lax.axis_index("gy").astype(F32) + 0.5
-    middle = jnp.stack([row, column, jnp.full_like(row, 0.5)] + [jnp.zeros_like(row)] * 5)
-    return jnp.broadcast_to(middle[:, None], (8, LEAF))
-
-
 def local(position, velocity, mass, pair_list, hot_leaf):
     pairs = to_slots(pair_list[0, 0], pair_list.shape[2])
     hot = hot_leaf[0, 0]
     half = 0.5 * time_step
-    origin = cell_origin()
-    speed = velocity[0, 0]
-    extended = surround(jnp.concatenate([position[0, 0], speed, mass[0, 0]], axis=0))
-    first_inverse, *first_kept = density(0.0, pairs, hot, extended, origin)
-    second_inverse, *second_kept = density(half, pairs, hot, extended, origin)
-    first = accel(0.0, pairs, hot, extended, surround(first_inverse), first_kept, origin)
-    mid_speed = speed + half * first
-    later = surround(jnp.concatenate([mid_speed, second_inverse], axis=0))
-    second = accel(half, pairs, hot, extended, later, second_kept, origin)
-    return ((time_step * mid_speed)[None, None], (speed + time_step * second)[None, None])
+    origin = jnp.stack([lax.axis_index("gx"), lax.axis_index("gy")]).astype(F32) + 0.5
+    extended = surround(jnp.concatenate([position[0, 0], velocity[0, 0], mass[0, 0]], axis=0))
+    inverse, kept = density(0.0, pairs, hot, origin, extended)
+    traded = swaps(inverse, "gx")
+    later_inverse, later_kept = density(half, pairs, hot, origin, extended)
+    *traded, later_inverse = lax.optimization_barrier((*traded, later_inverse))
+    here = jnp.stack([inverse] + traded)
+    inverses = [here] + swaps(here, "gy")
+    displacement, mid = accel(0.0, pairs, hot, origin, extended, inverses, kept, later_inverse)
+    new_velocity = accel(half, pairs, hot, origin, extended, surround(mid), later_kept)
+    return displacement.reshape(velocity.shape), new_velocity.reshape(velocity.shape)
 
 
 def solution(mesh):

time: 156 us -> 135 us (0.87)
  the two profiles are of different devices: /device:TPU:870 before, /device:TPU:313 now
where the time goes in v2:
time: 135 us; the launch traced here: 133 us
  starting transfers between devices  62 us (46%)
  Pallas kernels  37.6 us (28%)
  waiting for transfers between devices  29.6 us (22%)
  local copies, waits for them, and re-layouts  2.35 us (2%)
    ppermute x12, starting transfers between devices, swaps(): got.append(lax.ppermute(cells, axis, pairs + [(b, a) for a, b in pairs]))  62 us
    ppermute x12, waiting for transfers between devices, swaps(): got.append(lax.ppermute(cells, axis, pairs + [(b, a) for a, b in pairs]))  29.6 us
    pallas_call x2, Pallas kernels, accel(): pl.pallas_call(functools.partial(accel_kernel, drift, group, together), o...  21.7 us
    pallas_call x2, Pallas kernels, density(): pl.pallas_call(functools.partial(density_kernel, drift, group, together),...  15.9 us
  transfers between devices with their start and end apart: 12, of which 8 were waited for; matrix products, arithmetic and copies ran while one was open for 1% of the time, Pallas kernels for 6%

profile of v2, /device:TPU:313, one launch (start us, length us, event | category | flops | bytes accessed | tf_op | source)
XLA Modules:
  0.0 133.4 jit_solution(16615317539390796524)
XLA Ops:
  2.3 14.8 %collective-permute-start.1 = (f32[7,4096]{1,0:T(8,128)S(1)}, f32[7,4096]{1,0:T(8,128)S(1)}, u32[]{:S(2)}, u32[]{:S(2)}) collective-permute-start(f32[7,4096]{1,0:T(8,128)S(1)} %pad_maximum_fusion.2), channel_id=1, source_target_pairs={{32,64},{96,128},{160,192},{224,256},{288,320},{352,384},{416,448}... | collective-permute-start | bytes 344072 | tf_op jit(solution)/shard_map/ppermute | solution.py:273
  17.1 1.9 %collective-permute-start = (f32[7,4096]{1,0:T(8,128)S(1)}, f32[7,4096]{1,0:T(8,128)S(1)}, u32[]{:S(2)}, u32[]{:S(2)}) collective-permute-start(f32[7,4096]{1,0:T(8,128)S(1)} %pad_maximum_fusion.2), channel_id=1, source_target_pairs={{0,32},{64,96},{128,160},{192,224},{256,288},{320,352},{384,416},{... | collective-permute-start | bytes 344072 | tf_op jit(solution)/shard_map/ppermute | solution.py:273
  19.0 9.4 %collective-permute-done.1 = f32[7,4096]{1,0:T(8,128)S(1)} collective-permute-done((f32[7,4096]{1,0:T(8,128)S(1)}, f32[7,4096]{1,0:T(8,128)S(1)}, u32[]{:S(2)}, u32[]{:S(2)}) %collective-permute-start.1) | collective-permute-done | bytes 114720 | tf_op jit(solution)/shard_map/ppermute | solution.py:273
  28.4 6.0 %collective-permute-start.3 = (f32[3,7,4096]{2,1,0:T(8,128)S(1)}, f32[3,7,4096]{2,1,0:T(8,128)S(1)}, u32[]{:S(2)}, u32[]{:S(2)}) collective-permute-start(f32[3,7,4096]{2,1,0:T(8,128)S(1)} %pad_maximum_fusion.e_ref), channel_id=1, source_target_pairs={{1,2},{3,4},{5,6},{7,8},{9,10},{11,12},{13,14},{15,16},{17,18},{19... | collective-permute-start | bytes 1032200 | tf_op jit(solution)/shard_map/ppermute | solution.py:273
  34.4 1.9 %collective-permute-start.2 = (f32[3,7,4096]{2,1,0:T(8,128)S(1)}, f32[3,7,4096]{2,1,0:T(8,128)S(1)}, u32[]{:S(2)}, u32[]{:S(2)}) collective-permute-start(f32[3,7,4096]{2,1,0:T(8,128)S(1)} %pad_maximum_fusion.e_ref), channel_id=1, source_target_pairs={{0,1},{2,3},{4,5},{6,7},{8,9},{10,11},{12,13},{14,15},{16,17},{18,... | collective-permute-start | bytes 1032200 | tf_op jit(solution)/shard_map/ppermute | solution.py:273
  37.3 2.3 %collective-permute-done.3.e2_ref = f32[3,7,4096]{2,1,0:T(8,128)S(1)} collective-permute-done((f32[3,7,4096]{2,1,0:T(8,128)S(1)}, f32[3,7,4096]{2,1,0:T(8,128)S(1)}, u32[]{:S(2)}, u32[]{:S(2)}) %collective-permute-start.3) | collective-permute-done | bytes 344096 | tf_op jit(solution)/shard_map/ppermute | solution.py:273
  39.6 3.4 %collective-permute-done.2.e1_ref = f32[3,7,4096]{2,1,0:T(8,128)S(1)} collective-permute-done((f32[3,7,4096]{2,1,0:T(8,128)S(1)}, f32[3,7,4096]{2,1,0:T(8,128)S(1)}, u32[]{:S(2)}, u32[]{:S(2)}) %collective-permute-start.2) | collective-permute-done | bytes 344096 | tf_op jit(solution)/shard_map/ppermute | solution.py:273
  43.6 7.9 %density.2 = (f32[1,4096]{1,0:T(1,128)S(1)}, bf16[288,32,128]{2,1,0:T(8,128)(2,1)S(1)}) custom-call(s32[32,27]{1,0:T(8,128)S(1)} %fusion.pair_ref, s32[8]{0:T(128)S(1)} %bitcast.43, f32[2]{0:T(128)S(1)} %fusion.4.origin_ref, f32[3,7,4096]{2,1,0:T(8,128)S(1)} %pad_maximum_fusion.e_ref, f32[3,7,4096]{2,1,0:T(8,128)S(1)} %collective-permute-done.2.e1_ref, ...), custom_call_target="tpu_custom_call" | custom-call | tf_op jit(solution)/shard_map/density/pallas_call | solution.py:153
  51.5 15.0 %collective-permute-start.5 = (f32[1,4096]{1,0:T(1,128)S(1)}, f32[1,4096]{1,0:T(1,128)S(1)}, u32[]{:S(2)}, u32[]{:S(2)}) collective-permute-start(f32[1,4096]{1,0:T(1,128)S(1)} %get-tuple-element.11), channel_id=1, source_target_pairs={{32,64},{96,128},{160,192},{224,256},{288,320},{352,384},{416,448}... | collective-permute-start | bytes 49160 | tf_op jit(solution)/shard_map/ppermute | solution.py:273
  66.6 1.9 %collective-permute-start.4 = (f32[1,4096]{1,0:T(1,128)S(1)}, f32[1,4096]{1,0:T(1,128)S(1)}, u32[]{:S(2)}, u32[]{:S(2)}) collective-permute-start(f32[1,4096]{1,0:T(1,128)S(1)} %get-tuple-element.11), channel_id=1, source_target_pairs={{0,32},{64,96},{128,160},{192,224},{256,288},{320,352},{384,416},{... | collective-permute-start | bytes 49160 | tf_op jit(solution)/shard_map/ppermute | solution.py:273
  68.5 8.0 %density.3 = (f32[1,4096]{1,0:T(1,128)S(1)}, bf16[288,32,128]{2,1,0:T(8,128)(2,1)S(1)}) custom-call(s32[32,27]{1,0:T(8,128)S(1)} %fusion.pair_ref, s32[8]{0:T(128)S(1)} %bitcast.44, f32[2]{0:T(128)S(1)} %fusion.4.origin_ref, f32[3,7,4096]{2,1,0:T(8,128)S(1)} %pad_maximum_fusion.e_ref, f32[3,7,4096]{2,1,0:T(8,128)S(1)} %collective-permute-done.2.e1_ref, ...), custom_call_target="tpu_custom_call" | custom-call | tf_op jit(solution)/shard_map/density/pallas_call | solution.py:153
  76.6 3.0 %collective-permute-start.7 = (f32[3,1,4096]{2,1,0:T(1,128)S(1)}, f32[3,1,4096]{2,1,0:T(1,128)S(1)}, u32[]{:S(2)}, u32[]{:S(2)}) collective-permute-start(f32[3,1,4096]{2,1,0:T(1,128)S(1)} %pad_maximum_fusion.3.v_ref), channel_id=1, source_target_pairs={{1,2},{3,4},{5,6},{7,8},{9,10},{11,12},{13,14},{15,16},{17,18},{19... | collective-permute-start | bytes 147464 | tf_op jit(solution)/shard_map/ppermute | solution.py:273
  79.6 2.1 %collective-permute-start.6 = (f32[3,1,4096]{2,1,0:T(1,128)S(1)}, f32[3,1,4096]{2,1,0:T(1,128)S(1)}, u32[]{:S(2)}, u32[]{:S(2)}) collective-permute-start(f32[3,1,4096]{2,1,0:T(1,128)S(1)} %pad_maximum_fusion.3.v_ref), channel_id=1, source_target_pairs={{0,1},{2,3},{4,5},{6,7},{8,9},{10,11},{12,13},{14,15},{16,17},{18,... | collective-permute-start | bytes 147464 | tf_op jit(solution)/shard_map/ppermute | solution.py:273
  81.7 1.8 %collective-permute-done.7.v2_ref = f32[3,1,4096]{2,1,0:T(1,128)S(1)} collective-permute-done((f32[3,1,4096]{2,1,0:T(1,128)S(1)}, f32[3,1,4096]{2,1,0:T(1,128)S(1)}, u32[]{:S(2)}, u32[]{:S(2)}) %collective-permute-start.7) | collective-permute-done | bytes 49184 | tf_op jit(solution)/shard_map/ppermute | solution.py:273
  83.5 1.2 collective-permute-done.6.v1_ref
  84.8 10.7 %accel.2 = (f32[3,1,4096]{2,1,0:T(1,128)}, f32[4,4096]{1,0:T(4,128)S(1)}) custom-call(s32[32,27]{1,0:T(8,128)S(1)} %fusion.pair_ref, s32[8]{0:T(128)S(1)} %bitcast.45, f32[2]{0:T(128)S(1)} %fusion.4.origin_ref, f32[3,7,4096]{2,1,0:T(8,128)S(1)} %pad_maximum_fusion.e_ref, f32[3,7,4096]{2,1,0:T(8,128)S(1)} %collective-permute-done.2.e1_ref, ...), custom_call_target="tpu_custom_call" | custom-call | tf_op jit(solution)/shard_map/accel/pallas_call | solution.py:253
  95.5 7.0 %collective-permute-start.9 = (f32[4,4096]{1,0:T(4,128)S(1)}, f32[4,4096]{1,0:T(4,128)S(1)}, u32[]{:S(2)}, u32[]{:S(2)}) collective-permute-start(f32[4,4096]{1,0:T(4,128)S(1)} %get-tuple-element.18), channel_id=1, source_target_pairs={{32,64},{96,128},{160,192},{224,256},{288,320},{352,384},{416,448}... | collective-permute-start | bytes 196616 | tf_op jit(solution)/shard_map/ppermute | solution.py:273
  102.5 1.9 %collective-permute-start.8 = (f32[4,4096]{1,0:T(4,128)S(1)}, f32[4,4096]{1,0:T(4,128)S(1)}, u32[]{:S(2)}, u32[]{:S(2)}) collective-permute-start(f32[4,4096]{1,0:T(4,128)S(1)} %get-tuple-element.18), channel_id=1, source_target_pairs={{0,32},{64,96},{128,160},{192,224},{256,288},{320,352},{384,416},{... | collective-permute-start | bytes 196616 | tf_op jit(solution)/shard_map/ppermute | solution.py:273
  104.4 8.3 %collective-permute-done.9 = f32[4,4096]{1,0:T(4,128)S(1)} collective-permute-done((f32[4,4096]{1,0:T(4,128)S(1)}, f32[4,4096]{1,0:T(4,128)S(1)}, u32[]{:S(2)}, u32[]{:S(2)}) %collective-permute-start.9) | collective-permute-done | bytes 65568 | tf_op jit(solution)/shard_map/ppermute | solution.py:273
  112.8 3.2 %collective-permute-start.11 = (f32[3,4,4096]{2,1,0:T(4,128)S(1)}, f32[3,4,4096]{2,1,0:T(4,128)S(1)}, u32[]{:S(2)}, u32[]{:S(2)}) collective-permute-start(f32[3,4,4096]{2,1,0:T(4,128)S(1)} %pad_maximum_fusion.1.v_ref), channel_id=1, source_target_pairs={{1,2},{3,4},{5,6},{7,8},{9,10},{11,12},{13,14},{15,16},{17,18},{19... | collective-permute-start | bytes 589832 | tf_op jit(solution)/shard_map/ppermute | solution.py:273
  116.0 3.2 %collective-permute-start.10 = (f32[3,4,4096]{2,1,0:T(4,128)S(1)}, f32[3,4,4096]{2,1,0:T(4,128)S(1)}, u32[]{:S(2)}, u32[]{:S(2)}) collective-permute-start(f32[3,4,4096]{2,1,0:T(4,128)S(1)} %pad_maximum_fusion.1.v_ref), channel_id=1, source_target_pairs={{0,1},{2,3},{4,5},{6,7},{8,9},{10,11},{12,13},{14,15},{16,17},{18,... | collective-permute-start | bytes 589832 | tf_op jit(solution)/shard_map/ppermute | solution.py:273
  119.2 2.1 %collective-permute-done.11.v2_ref = f32[3,4,4096]{2,1,0:T(4,128)S(1)} collective-permute-done((f32[3,4,4096]{2,1,0:T(4,128)S(1)}, f32[3,4,4096]{2,1,0:T(4,128)S(1)}, u32[]{:S(2)}, u32[]{:S(2)}) %collective-permute-start.11) | collective-permute-done | bytes 196640 | tf_op jit(solution)/shard_map/ppermute | solution.py:273
  121.3 1.1 collective-permute-done.10.v1_ref
  122.4 11.0 %accel.3 = f32[3,1,4096]{2,1,0:T(1,128)} custom-call(s32[32,27]{1,0:T(8,128)S(1)} %fusion.pair_ref, s32[8]{0:T(128)S(1)} %bitcast.46, f32[2]{0:T(128)S(1)} %fusion.4.origin_ref, f32[3,7,4096]{2,1,0:T(8,128)S(1)} %pad_maximum_fusion.e_ref, f32[3,7,4096]{2,1,0:T(8,128)S(1)} %collective-permute-done.2.e1_ref, f32[3,7,4096]{2,1,0:T(8,128)S(1)} %collective-permute-done.3.e2_ref, ...), custom_call_target="tpu_custom_call" | custom-call | tf_op jit(solution)/shard_map/accel/pallas_call | solution.py:253
  (16 shorter events, 3.4 us)
Async XLA Ops:
  0.6 67.9 %copy-start.1 = (s32[1,1,8]{2,1,0:T(1,128)S(1)}, s32[1,1,8]{2,1,0:T(1,128)}, u32[]{:S(2)}) copy-start(s32[1,1,8]{2,1,0:T(1,128)} %param.9) | copy-start | bytes 100
  2.3 26.1 %collective-permute-start.1 = (f32[7,4096]{1,0:T(8,128)S(1)}, f32[7,4096]{1,0:T(8,128)S(1)}, u32[]{:S(2)}, u32[]{:S(2)}) collective-permute-start(f32[7,4096]{1,0:T(8,128)S(1)} %pad_maximum_fusion.2), channel_id=1, source_target_pairs={{32,64},{96,128},{160,192},{224,256},{288,320},{352,384},{416,448}... | collective-permute-start | bytes 344072 | tf_op jit(solution)/shard_map/ppermute | solution.py:273
  17.1 11.3 %collective-permute-start = (f32[7,4096]{1,0:T(8,128)S(1)}, f32[7,4096]{1,0:T(8,128)S(1)}, u32[]{:S(2)}, u32[]{:S(2)}) collective-permute-start(f32[7,4096]{1,0:T(8,128)S(1)} %pad_maximum_fusion.2), channel_id=1, source_target_pairs={{0,32},{64,96},{128,160},{192,224},{256,288},{320,352},{384,416},{... | collective-permute-start | bytes 344072 | tf_op jit(solution)/shard_map/ppermute | solution.py:273
  28.4 11.2 %collective-permute-start.3 = (f32[3,7,4096]{2,1,0:T(8,128)S(1)}, f32[3,7,4096]{2,1,0:T(8,128)S(1)}, u32[]{:S(2)}, u32[]{:S(2)}) collective-permute-start(f32[3,7,4096]{2,1,0:T(8,128)S(1)} %pad_maximum_fusion.e_ref), channel_id=1, source_target_pairs={{1,2},{3,4},{5,6},{7,8},{9,10},{11,12},{13,14},{15,16},{17,18},{19... | collective-permute-start | bytes 1032200 | tf_op jit(solution)/shard_map/ppermute | solution.py:273
  34.4 8.5 %collective-permute-start.2 = (f32[3,7,4096]{2,1,0:T(8,128)S(1)}, f32[3,7,4096]{2,1,0:T(8,128)S(1)}, u32[]{:S(2)}, u32[]{:S(2)}) collective-permute-start(f32[3,7,4096]{2,1,0:T(8,128)S(1)} %pad_maximum_fusion.e_ref), channel_id=1, source_target_pairs={{0,1},{2,3},{4,5},{6,7},{8,9},{10,11},{12,13},{14,15},{16,17},{18,... | collective-permute-start | bytes 1032200 | tf_op jit(solution)/shard_map/ppermute | solution.py:273
  43.0 0.7 copy-start
  51.5 25.0 %collective-permute-start.5 = (f32[1,4096]{1,0:T(1,128)S(1)}, f32[1,4096]{1,0:T(1,128)S(1)}, u32[]{:S(2)}, u32[]{:S(2)}) collective-permute-start(f32[1,4096]{1,0:T(1,128)S(1)} %get-tuple-element.11), channel_id=1, source_target_pairs={{32,64},{96,128},{160,192},{224,256},{288,320},{352,384},{416,448}... | collective-permute-start | bytes 49160 | tf_op jit(solution)/shard_map/ppermute | solution.py:273
  66.6 10.0 %collective-permute-start.4 = (f32[1,4096]{1,0:T(1,128)S(1)}, f32[1,4096]{1,0:T(1,128)S(1)}, u32[]{:S(2)}, u32[]{:S(2)}) collective-permute-start(f32[1,4096]{1,0:T(1,128)S(1)} %get-tuple-element.11), channel_id=1, source_target_pairs={{0,32},{64,96},{128,160},{192,224},{256,288},{320,352},{384,416},{... | collective-permute-start | bytes 49160 | tf_op jit(solution)/shard_map/ppermute | solution.py:273
  76.6 6.9 %collective-permute-start.7 = (f32[3,1,4096]{2,1,0:T(1,128)S(1)}, f32[3,1,4096]{2,1,0:T(1,128)S(1)}, u32[]{:S(2)}, u32[]{:S(2)}) collective-permute-start(f32[3,1,4096]{2,1,0:T(1,128)S(1)} %pad_maximum_fusion.3.v_ref), channel_id=1, source_target_pairs={{1,2},{3,4},{5,6},{7,8},{9,10},{11,12},{13,14},{15,16},{17,18},{19... | collective-permute-start | bytes 147464 | tf_op jit(solution)/shard_map/ppermute | solution.py:273
  79.6 5.1 %collective-permute-start.6 = (f32[3,1,4096]{2,1,0:T(1,128)S(1)}, f32[3,1,4096]{2,1,0:T(1,128)S(1)}, u32[]{:S(2)}, u32[]{:S(2)}) collective-permute-start(f32[3,1,4096]{2,1,0:T(1,128)S(1)} %pad_maximum_fusion.3.v_ref), channel_id=1, source_target_pairs={{0,1},{2,3},{4,5},{6,7},{8,9},{10,11},{12,13},{14,15},{16,17},{18,... | collective-permute-start | bytes 147464 | tf_op jit(solution)/shard_map/ppermute | solution.py:273
  95.5 17.3 %collective-permute-start.9 = (f32[4,4096]{1,0:T(4,128)S(1)}, f32[4,4096]{1,0:T(4,128)S(1)}, u32[]{:S(2)}, u32[]{:S(2)}) collective-permute-start(f32[4,4096]{1,0:T(4,128)S(1)} %get-tuple-element.18), channel_id=1, source_target_pairs={{32,64},{96,128},{160,192},{224,256},{288,320},{352,384},{416,448}... | collective-permute-start | bytes 196616 | tf_op jit(solution)/shard_map/ppermute | solution.py:273
  102.5 10.3 %collective-permute-start.8 = (f32[4,4096]{1,0:T(4,128)S(1)}, f32[4,4096]{1,0:T(4,128)S(1)}, u32[]{:S(2)}, u32[]{:S(2)}) collective-permute-start(f32[4,4096]{1,0:T(4,128)S(1)} %get-tuple-element.18), channel_id=1, source_target_pairs={{0,32},{64,96},{128,160},{192,224},{256,288},{320,352},{384,416},{... | collective-permute-start | bytes 196616 | tf_op jit(solution)/shard_map/ppermute | solution.py:273
  112.8 8.5 %collective-permute-start.11 = (f32[3,4,4096]{2,1,0:T(4,128)S(1)}, f32[3,4,4096]{2,1,0:T(4,128)S(1)}, u32[]{:S(2)}, u32[]{:S(2)}) collective-permute-start(f32[3,4,4096]{2,1,0:T(4,128)S(1)} %pad_maximum_fusion.1.v_ref), channel_id=1, source_target_pairs={{1,2},{3,4},{5,6},{7,8},{9,10},{11,12},{13,14},{15,16},{17,18},{19... | collective-permute-start | bytes 589832 | tf_op jit(solution)/shard_map/ppermute | solution.py:273
  116.0 6.4 %collective-permute-start.10 = (f32[3,4,4096]{2,1,0:T(4,128)S(1)}, f32[3,4,4096]{2,1,0:T(4,128)S(1)}, u32[]{:S(2)}, u32[]{:S(2)}) collective-permute-start(f32[3,4,4096]{2,1,0:T(4,128)S(1)} %pad_maximum_fusion.1.v_ref), channel_id=1, source_target_pairs={{0,1},{2,3},{4,5},{6,7},{8,9},{10,11},{12,13},{14,15},{16,17},{18,... | collective-permute-start | bytes 589832 | tf_op jit(solution)/shard_map/ppermute | solution.py:273
